TPU v7x, 32 devices: a whole 2x2x4 slice. The times are simulated.
32 devices in a mesh: job: 2 (over y), dp: 4 (over x, core), panel: 4 (over z).
Axes of the slice: x: 2, y: 2, z: 4, core: 2. Of those that a mesh axis runs over, the one named last changes fastest.
Arguments:
- acts: bfloat16 [4096, 8192], P(('job', 'dp')), parts along dimension 0, may hold values from -6 to 6
- cotangent: bfloat16 [4096, 28672], P(('job', 'dp'), 'panel'), parts along dimension 0, may hold values from -0.3125 to 0.3125
- down_factor_rows: bfloat16 [32, 8192], P('job'), parts along dimension 0, may hold values from -0.0625 to 0.0625
- up_factor_matrix: bfloat16 [32, 28672], P('job', 'panel'), parts along dimension 0, may hold values from -0.03125 to 0.03125
- slot_block_rows: int32 [8, 8], P(('job', 'panel')), parts along dimension 0, may hold values from 0 to 63, as said below
- panel_block_columns: int32 [8, 8], P(('job', 'panel')), parts along dimension 0, may hold values from 0 to 55, as said below
- panel_live_count: int32 [8], P(('job', 'panel')), parts along dimension 0, may hold values from 2 to 8, as said below
Outputs:
- block_grads: float32 [8, 8, 128, 128], P(('job', 'panel'), 'dp'), parts along dimension 0
- grad_down: float32 [32, 8192], P('job', 'panel'), parts along dimension 0
- grad_up: float32 [32, 28672], P('job', 'panel'), parts along dimension 0
There are 2 independent parts, one for each index of `job`. A program takes and returns all parts, laid end to end along the dimension named above; each array names one. Nothing has to cross between parts.
Inputs may be any that keep to these rules, and one draw needn't show every extreme that they name: `slot_block_rows`: row block indices of the slots. Column block indices within the panel; within one panel the 8 pairs (slot_block_rows, panel_block_columns) are all different. Only the first panel_live_count[p] slots of panel p are live; some panel has all 8 slots live.
All inputs are finite; a program needn't handle non-finite values.
Results may differ from a plain program's by a relative error of at most 0.0029.
Values may be sent and summed in bfloat16 or wider, within the bound.
No kernel may reach another device: no remote copies, remote signals or barrier semaphores. Data moves between devices by JAX's collectives and lax.ppermute only.
A program may use at most 128 MiB of HBM per device.

v0:
```python
import jax
import jax.numpy as jnp
from jax import lax
from jax.sharding import PartitionSpec as P

BLK = 128


def pick_blocks(matrix, block_ids):

    def one_block(block_id):
        return lax.dynamic_slice_in_dim(matrix, block_id * BLK, BLK, 1)

    return jax.vmap(one_block)(block_ids)


def pair_products(pair_blocks):
    return jnp.einsum(
        "usta,ustb->sab", pair_blocks[0], pair_blocks[1], preferred_element_type=jnp.float32
    )


def body(
    acts,
    cotangent,
    down_factor_rows,
    up_factor_matrix,
    slot_block_rows,
    panel_block_columns,
    panel_live_count,
):
    slot_rows = slot_block_rows[0]
    slot_cols = panel_block_columns[0]
    live_count = panel_live_count[0]
    local_tokens = acts.shape[0]
    dp_count = lax.axis_size("dp")
    slot_dev = slot_rows.shape[0] // dp_count
    act_picked = pick_blocks(acts, slot_rows).reshape(dp_count, slot_dev, local_tokens, BLK)
    cot_picked = pick_blocks(cotangent, slot_cols).reshape(dp_count, slot_dev, local_tokens, BLK)
    stacked = jnp.stack([act_picked, cot_picked])
    block_sums = pair_products(
        lax.all_to_all(stacked, "dp", split_axis=1, concat_axis=3, tiled=True)
    )
    first_slot = lax.axis_index("dp") * slot_dev
    live_slots = first_slot + jnp.arange(slot_dev, dtype=jnp.int32) < live_count
    block_grads = jnp.where(live_slots[:, None, None], block_sums, jnp.float32(0.0))[None]
    contract_final_axis = (((1,), (1,)), ((), ()))
    contract_first = (((0,), (0,)), ((), ()))
    lowrank_input = lax.dot_general(
        acts, down_factor_rows, contract_final_axis, preferred_element_type=jnp.float32
    ).astype(jnp.bfloat16)
    grad_up_part = lax.dot_general(
        lowrank_input, cotangent, contract_first, preferred_element_type=jnp.float32
    )
    back_part = lax.dot_general(
        cotangent, up_factor_matrix, contract_final_axis, preferred_element_type=jnp.float32
    )
    backward_projection = lax.psum(back_part, "panel").astype(jnp.bfloat16)
    slice_width = acts.shape[1] // lax.axis_size("panel")
    down_full = lax.dot_general(
        backward_projection, acts, contract_first, preferred_element_type=jnp.float32
    )
    grad_down_part = lax.dynamic_slice_in_dim(
        down_full, lax.axis_index("panel") * slice_width, slice_width, 1
    )
    grad_down, grad_up = lax.psum((grad_down_part, grad_up_part), "dp")
    return (block_grads, grad_down, grad_up)


def solution(mesh):
    in_specs = (
        P(("job", "dp"), None),
        P(("job", "dp"), "panel"),
        P("job", None),
        P("job", "panel"),
        P(("job", "panel"), None),
        P(("job", "panel"), None),
        P(("job", "panel")),
    )
    out_specs = (P(("job", "panel"), "dp", None, None), P("job", "panel"), P("job", "panel"))
    return jax.shard_map(body, mesh=mesh, in_specs=in_specs, out_specs=out_specs, check_vma=False)
```

profile of v0, /device:TPU:0, one launch (start us, length us, event | category | flops | bytes accessed | tf_op | source)
XLA Modules:
  0.0 142.6 jit_solution(6280654867166648106)
XLA Ops:
  7.2 0.7 compare_select_fusion
  8.1 18.7 %while.3 = (s32[]{:T(128)}, bf16[512,7168]{1,0:T(8,128)(2,1)}, s32[8,2]{0,1:T(2,128)S(1)}, bf16[8,512,128]{2,1,0:T(8,128)(2,1)S(1)}, s32[]{:T(128)}) while((s32[]{:T(128)}, bf16[512,7168]{1,0:T(8,128)(2,1)}, s32[8,2]{0,1:T(2,128)S(1)}, bf16[8,512,128]{2,1,0:T(8,128)(2,1)S(1)}, s32[]{:T(128)}) %tuple.32), condition=%wide.while_cond.1, body=%wide.while_body.1.sunk | while | flops 2 | bytes 262249 | solution.py:12
  8.2 0.5 slice.39
  8.7 1.7 %bitcast_dynamic-update-slice_fusion.5 = bf16[8,512,128]{2,1,0:T(8,128)(2,1)S(1)} fusion(bf16[8,512,128]{2,1,0:T(8,128)(2,1)S(1)} %get-tuple-element.97, s32[]{:T(128)S(6)} %copy.19, bf16[512,7168]{1,0:T(8,128)(2,1)} %get-tuple-element.100, s32[]{:T(128)} %bitcast.37), kind=kLoop, calls=%fused_computation.2.clone.1 | loop fusion | bytes 262152 | tf_op jit(solution)/shard_map/vmap()/gather
  10.5 0.5 slice.39
  11.0 1.7 %bitcast_dynamic-update-slice_fusion.5 = bf16[8,512,128]{2,1,0:T(8,128)(2,1)S(1)} fusion(bf16[8,512,128]{2,1,0:T(8,128)(2,1)S(1)} %get-tuple-element.97, s32[]{:T(128)S(6)} %copy.19, bf16[512,7168]{1,0:T(8,128)(2,1)} %get-tuple-element.100, s32[]{:T(128)} %bitcast.37), kind=kLoop, calls=%fused_computation.2.clone.1 | loop fusion | bytes 262152 | tf_op jit(solution)/shard_map/vmap()/gather
  12.8 0.5 slice.39
  13.3 1.7 %bitcast_dynamic-update-slice_fusion.5 = bf16[8,512,128]{2,1,0:T(8,128)(2,1)S(1)} fusion(bf16[8,512,128]{2,1,0:T(8,128)(2,1)S(1)} %get-tuple-element.97, s32[]{:T(128)S(6)} %copy.19, bf16[512,7168]{1,0:T(8,128)(2,1)} %get-tuple-element.100, s32[]{:T(128)} %bitcast.37), kind=kLoop, calls=%fused_computation.2.clone.1 | loop fusion | bytes 262152 | tf_op jit(solution)/shard_map/vmap()/gather
  15.2 0.5 slice.39
  15.7 1.7 %bitcast_dynamic-update-slice_fusion.5 = bf16[8,512,128]{2,1,0:T(8,128)(2,1)S(1)} fusion(bf16[8,512,128]{2,1,0:T(8,128)(2,1)S(1)} %get-tuple-element.97, s32[]{:T(128)S(6)} %copy.19, bf16[512,7168]{1,0:T(8,128)(2,1)} %get-tuple-element.100, s32[]{:T(128)} %bitcast.37), kind=kLoop, calls=%fused_computation.2.clone.1 | loop fusion | bytes 262152 | tf_op jit(solution)/shard_map/vmap()/gather
  17.5 0.5 slice.39
  18.0 1.7 %bitcast_dynamic-update-slice_fusion.5 = bf16[8,512,128]{2,1,0:T(8,128)(2,1)S(1)} fusion(bf16[8,512,128]{2,1,0:T(8,128)(2,1)S(1)} %get-tuple-element.97, s32[]{:T(128)S(6)} %copy.19, bf16[512,7168]{1,0:T(8,128)(2,1)} %get-tuple-element.100, s32[]{:T(128)} %bitcast.37), kind=kLoop, calls=%fused_computation.2.clone.1 | loop fusion | bytes 262152 | tf_op jit(solution)/shard_map/vmap()/gather
  19.8 0.5 slice.39
  20.4 1.7 %bitcast_dynamic-update-slice_fusion.5 = bf16[8,512,128]{2,1,0:T(8,128)(2,1)S(1)} fusion(bf16[8,512,128]{2,1,0:T(8,128)(2,1)S(1)} %get-tuple-element.97, s32[]{:T(128)S(6)} %copy.19, bf16[512,7168]{1,0:T(8,128)(2,1)} %get-tuple-element.100, s32[]{:T(128)} %bitcast.37), kind=kLoop, calls=%fused_computation.2.clone.1 | loop fusion | bytes 262152 | tf_op jit(solution)/shard_map/vmap()/gather
  22.2 0.5 slice.39
  22.7 1.7 %bitcast_dynamic-update-slice_fusion.5 = bf16[8,512,128]{2,1,0:T(8,128)(2,1)S(1)} fusion(bf16[8,512,128]{2,1,0:T(8,128)(2,1)S(1)} %get-tuple-element.97, s32[]{:T(128)S(6)} %copy.19, bf16[512,7168]{1,0:T(8,128)(2,1)} %get-tuple-element.100, s32[]{:T(128)} %bitcast.37), kind=kLoop, calls=%fused_computation.2.clone.1 | loop fusion | bytes 262152 | tf_op jit(solution)/shard_map/vmap()/gather
  24.5 0.5 slice.39
  25.0 1.7 %bitcast_dynamic-update-slice_fusion.5 = bf16[8,512,128]{2,1,0:T(8,128)(2,1)S(1)} fusion(bf16[8,512,128]{2,1,0:T(8,128)(2,1)S(1)} %get-tuple-element.97, s32[]{:T(128)S(6)} %copy.19, bf16[512,7168]{1,0:T(8,128)(2,1)} %get-tuple-element.100, s32[]{:T(128)} %bitcast.37), kind=kLoop, calls=%fused_computation.2.clone.1 | loop fusion | bytes 262152 | tf_op jit(solution)/shard_map/vmap()/gather
  26.8 0.7 compare_select_fusion.1
  27.6 18.7 %while.2 = (s32[]{:T(128)}, bf16[512,8192]{1,0:T(8,128)(2,1)}, s32[8,2]{0,1:T(2,128)S(1)}, bf16[8,512,128]{2,1,0:T(8,128)(2,1)S(1)}, s32[]{:T(128)}) while((s32[]{:T(128)}, bf16[512,8192]{1,0:T(8,128)(2,1)}, s32[8,2]{0,1:T(2,128)S(1)}, bf16[8,512,128]{2,1,0:T(8,128)(2,1)S(1)}, s32[]{:T(128)}) %tuple.35), condition=%wide.while_cond, body=%wide.while_body.sunk | while | flops 2 | bytes 262249 | solution.py:12
  27.7 0.5 slice.38
  28.2 1.7 %bitcast_dynamic-update-slice_fusion.4 = bf16[8,512,128]{2,1,0:T(8,128)(2,1)S(1)} fusion(bf16[8,512,128]{2,1,0:T(8,128)(2,1)S(1)} %get-tuple-element.112, s32[]{:T(128)S(6)} %copy.25, bf16[512,8192]{1,0:T(8,128)(2,1)} %get-tuple-element.115, s32[]{:T(128)} %bitcast.35), kind=kLoop, calls=%fused_computation.clone.1 | loop fusion | bytes 262152 | tf_op jit(solution)/shard_map/vmap()/gather
  30.0 0.5 slice.38
  30.5 1.7 %bitcast_dynamic-update-slice_fusion.4 = bf16[8,512,128]{2,1,0:T(8,128)(2,1)S(1)} fusion(bf16[8,512,128]{2,1,0:T(8,128)(2,1)S(1)} %get-tuple-element.112, s32[]{:T(128)S(6)} %copy.25, bf16[512,8192]{1,0:T(8,128)(2,1)} %get-tuple-element.115, s32[]{:T(128)} %bitcast.35), kind=kLoop, calls=%fused_computation.clone.1 | loop fusion | bytes 262152 | tf_op jit(solution)/shard_map/vmap()/gather
  32.9 1.7 %bitcast_dynamic-update-slice_fusion.4 = bf16[8,512,128]{2,1,0:T(8,128)(2,1)S(1)} fusion(bf16[8,512,128]{2,1,0:T(8,128)(2,1)S(1)} %get-tuple-element.112, s32[]{:T(128)S(6)} %copy.25, bf16[512,8192]{1,0:T(8,128)(2,1)} %get-tuple-element.115, s32[]{:T(128)} %bitcast.35), kind=kLoop, calls=%fused_computation.clone.1 | loop fusion | bytes 262152 | tf_op jit(solution)/shard_map/vmap()/gather
  34.7 0.5 slice.38
  35.2 1.7 %bitcast_dynamic-update-slice_fusion.4 = bf16[8,512,128]{2,1,0:T(8,128)(2,1)S(1)} fusion(bf16[8,512,128]{2,1,0:T(8,128)(2,1)S(1)} %get-tuple-element.112, s32[]{:T(128)S(6)} %copy.25, bf16[512,8192]{1,0:T(8,128)(2,1)} %get-tuple-element.115, s32[]{:T(128)} %bitcast.35), kind=kLoop, calls=%fused_computation.clone.1 | loop fusion | bytes 262152 | tf_op jit(solution)/shard_map/vmap()/gather
  37.0 0.5 slice.38
  37.5 1.7 %bitcast_dynamic-update-slice_fusion.4 = bf16[8,512,128]{2,1,0:T(8,128)(2,1)S(1)} fusion(bf16[8,512,128]{2,1,0:T(8,128)(2,1)S(1)} %get-tuple-element.112, s32[]{:T(128)S(6)} %copy.25, bf16[512,8192]{1,0:T(8,128)(2,1)} %get-tuple-element.115, s32[]{:T(128)} %bitcast.35), kind=kLoop, calls=%fused_computation.clone.1 | loop fusion | bytes 262152 | tf_op jit(solution)/shard_map/vmap()/gather
  39.3 0.5 slice.38
  39.9 1.7 %bitcast_dynamic-update-slice_fusion.4 = bf16[8,512,128]{2,1,0:T(8,128)(2,1)S(1)} fusion(bf16[8,512,128]{2,1,0:T(8,128)(2,1)S(1)} %get-tuple-element.112, s32[]{:T(128)S(6)} %copy.25, bf16[512,8192]{1,0:T(8,128)(2,1)} %get-tuple-element.115, s32[]{:T(128)} %bitcast.35), kind=kLoop, calls=%fused_computation.clone.1 | loop fusion | bytes 262152 | tf_op jit(solution)/shard_map/vmap()/gather
  41.7 0.5 slice.38
  42.2 1.7 %bitcast_dynamic-update-slice_fusion.4 = bf16[8,512,128]{2,1,0:T(8,128)(2,1)S(1)} fusion(bf16[8,512,128]{2,1,0:T(8,128)(2,1)S(1)} %get-tuple-element.112, s32[]{:T(128)S(6)} %copy.25, bf16[512,8192]{1,0:T(8,128)(2,1)} %get-tuple-element.115, s32[]{:T(128)} %bitcast.35), kind=kLoop, calls=%fused_computation.clone.1 | loop fusion | bytes 262152 | tf_op jit(solution)/shard_map/vmap()/gather
  44.5 1.7 %bitcast_dynamic-update-slice_fusion.4 = bf16[8,512,128]{2,1,0:T(8,128)(2,1)S(1)} fusion(bf16[8,512,128]{2,1,0:T(8,128)(2,1)S(1)} %get-tuple-element.112, s32[]{:T(128)S(6)} %copy.25, bf16[512,8192]{1,0:T(8,128)(2,1)} %get-tuple-element.115, s32[]{:T(128)} %bitcast.35), kind=kLoop, calls=%fused_computation.clone.1 | loop fusion | bytes 262152 | tf_op jit(solution)/shard_map/vmap()/gather
  46.3 1.5 %pad_maximum_fusion = bf16[2,4,2,512,128]{4,3,2,0,1:T(8,128)(2,1)} fusion(bf16[1,4,2,512,128]{4,3,2,0,1:T(8,128)(2,1)S(1)} %bitcast.42, bf16[1,4,2,512,128]{4,3,2,0,1:T(8,128)(2,1)S(1)} %bitcast.41), kind=kLoop, calls=%fused_computation.4 | loop fusion | flops 1048576 | bytes 4194304 | tf_op jit(solution)/shard_map/stack | solution.py:40
  47.8 4.2 %all-to-all-start = ((bf16[2,4,2,512,128]{4,3,2,0,1:T(8,128)(2,1)}), bf16[2,4,2,512,128]{4,3,2,0,1:T(8,128)(2,1)S(1)}, u32[]{:S(2)}, u32[]{:S(2)}) async-start(bf16[2,4,2,512,128]{4,3,2,0,1:T(8,128)(2,1)} %pad_maximum_fusion), calls=%async_computation | async-start | bytes 4194304 | tf_op jit(solution)/shard_map/all_to_all | solution.py:42
  52.0 5.1 %fusion.5 = f32[512,16]{1,0:T(8,128)S(1)} fusion(bf16[512,7168]{1,0:T(8,128)(2,1)} %get-tuple-element.127, bf16[16,7168]{1,0:T(8,128)(2,1)S(1)} %copy-done.1), kind=kOutput, calls=%fused_computation.16 | convolution fusion | flops 117440512 | bytes 7602176 | tf_op jit(solution)/shard_map/dot_general | solution.py:55
  57.1 25.8 %psum.21 = bf16[512,16]{1,0:T(8,128)(2,1)S(1)} all-reduce(f32[512,16]{1,0:T(8,128)S(1)} %fusion.5), channel_id=1, replica_groups=mesh['job'=2,'dp'=4,'panel'=4] {'panel'}, use_global_device_ids=true, to_apply=%region_0.1 | all-reduce | flops 8192 | bytes 49152 | tf_op jit(solution)/shard_map/psum | solution.py:58
  83.0 4.6 %fusion.6 = f32[16,8192]{1,0:T(8,128)S(1)} fusion(bf16[512,16]{1,0:T(8,128)(2,1)S(1)} %psum.21, bf16[512,8192]{1,0:T(8,128)(2,1)} %get-tuple-element.126), kind=kOutput, calls=%fused_computation.17 | convolution fusion | flops 134217728 | bytes 8929280 | tf_op jit(solution)/shard_map/dot_general | solution.py:60
  87.6 0.7 constant_dynamic-slice_fusion.2
  88.3 11.4 %fusion = f32[16,7168]{1,0:T(8,128)} fusion(bf16[512,7168]{1,0:T(8,128)(2,1)} %get-tuple-element.127, bf16[512,8192]{1,0:T(8,128)(2,1)} %get-tuple-element.126, bf16[16,8192]{1,0:T(8,128)(2,1)S(1)} %copy-done), kind=kOutput, calls=%fused_computation.6 | convolution fusion | flops 251666432 | bytes 16449536 | tf_op jit(solution)/shard_map/dot_general | solution.py:52
  100.4 1.1 fusion.4
  101.5 1.9 %copy.13 = bf16[1,1,2,4,512,128]{4,3,5,2,1,0:T(4,128)(2,1)S(1)} copy(bf16[1,1,2,4,512,128]{5,4,2,0,3,1:T(8,128)(2,1)} %get-tuple-element.38) | data formatting | bytes 2097152 | tf_op jit(solution)/shard_map/slice | solution.py:19
  103.4 0.8 reshape.65
  104.3 1.1 fusion.1
  105.4 27.0 %all-reduce.5.cloned.1.call-done = (f32[16,2048]{1,0:T(8,128)}, f32[16,7168]{1,0:T(8,128)}) async-done(((f32[16,2048]{1,0:T(8,128)}, f32[16,7168]{1,0:T(8,128)}), (f32[16,2048]{1,0:T(8,128)}, f32[16,7168]{1,0:T(8,128)})) %all-reduce.5.cloned.1.call-update) | async-done | bytes 589840 | tf_op jit(solution)/shard_map/psum | solution.py:66
  132.4 1.6 %copy.32 = f32[16,2048]{1,0:T(8,128)} copy(f32[16,2048]{1,0:T(8,128)} %get-tuple-element.120) | data formatting | bytes 262144
  133.9 1.8 %copy.33 = f32[16,7168]{1,0:T(8,128)} copy(f32[16,7168]{1,0:T(8,128)} %get-tuple-element.121) | data formatting | bytes 917504
  (31 shorter events, 2.6 us)
Async XLA Ops:
  7.2 81.1 %copy-start = (bf16[16,8192]{1,0:T(8,128)(2,1)S(1)}, bf16[16,8192]{1,0:T(8,128)(2,1)}, u32[]{:S(2)}) copy-start(bf16[16,8192]{1,0:T(8,128)(2,1)} %param.9) | copy-start | bytes 786436
  7.2 44.8 %copy-start.1 = (bf16[16,7168]{1,0:T(8,128)(2,1)S(1)}, bf16[16,7168]{1,0:T(8,128)(2,1)}, u32[]{:S(2)}) copy-start(bf16[16,7168]{1,0:T(8,128)(2,1)} %param.10) | copy-start | bytes 688132
  47.8 52.6 %all-to-all-start = ((bf16[2,4,2,512,128]{4,3,2,0,1:T(8,128)(2,1)}), bf16[2,4,2,512,128]{4,3,2,0,1:T(8,128)(2,1)S(1)}, u32[]{:S(2)}, u32[]{:S(2)}) async-start(bf16[2,4,2,512,128]{4,3,2,0,1:T(8,128)(2,1)} %pad_maximum_fusion), calls=%async_computation | async-start | bytes 4194304 | tf_op jit(solution)/shard_map/all_to_all | solution.py:42
  52.0 80.3 %all-reduce.5.cloned.1.call-start = ((), (), s32[]{:S(2)}) async-start(), calls=%async_computation.1 | async-start | bytes 1179648 | tf_op jit(solution)/shard_map/psum | solution.py:66
Sparse Core Ops, SparseCore 0:
  99.8 32.4 all-reduce.4
where the time goes:
time: 144 us; the launch traced here: 143 us
  local copies, waits for them, and re-layouts  45.3 us (31%)
  waiting for transfers between devices  27 us (19%)
  blocking collectives  25.8 us (18%)
  matrix products  22.2 us (15%)
  between operations  14.8 us (10%)
  starting transfers between devices  4.21 us (3%)
  other arithmetic  2.93 us (2%)
    gather x48, local copies, waits for them, and re-layouts  37.1 us
    psum x1, waiting for transfers between devices, body(): grad_down, grad_up = lax.psum((grad_down_part, grad_up_part), 'dp')  27 us
    psum x1, blocking collectives, body(): backward_projection = lax.psum(back_part, 'panel').astype(jnp.bfloat16)  25.8 us
    dot_general x1, matrix products, body(): lax.dot_general(lowrank_input, cotangent, contract_first, preferred_eleme...  11.4 us
    dot_general x1, matrix products, body(): lax.dot_general(cotangent, up_factor_matrix, contract_final_axis, preferr...  5.11 us
    dot_general x1, matrix products, body(): lax.dot_general(backward_projection, acts, contract_first, preferred_elem...  4.6 us
    all_to_all x1, starting transfers between devices, body(): lax.all_to_all(stacked, 'dp', split_axis=1, concat_axis=3, tiled=True)  4.21 us
    unnamed x8, local copies, waits for them, and re-layouts  3.67 us
  transfers between devices with their start and end apart: 2, of which 1 were waited for; matrix products, arithmetic and copies ran while one was open for 19% of the time, Pallas kernels for 0%

commit v1 on v0

v1 whole, which is shorter than its diff:
```python
import functools

import jax
import jax.numpy as jnp
from jax import lax
from jax.experimental import pallas as pl
from jax.experimental.pallas import tpu as pltpu
from jax.sharding import PartitionSpec as P

BLK = 128
COT_CHUNK = 512
ACT_CHUNK = 1024
LAST_LAST = (((1,), (1,)), ((), ()))
LAST_FIRST = (((1,), (0,)), ((), ()))
FIRST_FIRST = (((0,), (0,)), ((), ()))
IN_HBM = pl.BlockSpec(memory_space=pltpu.HBM)
IN_VMEM = pl.BlockSpec(memory_space=pltpu.VMEM)
IN_SMEM = pl.BlockSpec(memory_space=pltpu.SMEM)


def dot(a, b, dims):
    return lax.dot_general(a, b, dims, preferred_element_type=jnp.float32)


def call(kernel, outs, specs, args, scratch=(), flops=0, moved=0):
    return pl.pallas_call(
        kernel,
        out_shape=outs,
        in_specs=specs,
        out_specs=jax.tree.map(lambda _: IN_VMEM, outs),
        scratch_shapes=scratch,
        cost_estimate=pl.CostEstimate(flops=flops, bytes_accessed=moved, transcendentals=0),
        compiler_params=pltpu.CompilerParams(vmem_limit_bytes=16 * 2**20),
    )(*args)


def back_kernel(cot, up, back, cot_here, up_here, sems):
    width = cot.shape[1]
    step = min(COT_CHUNK, width)
    count = width // step
    first = pltpu.make_async_copy(up, up_here, sems.at[count])
    first.start()
    copies = []
    for j in range(count):
        cols = pl.ds(j * step, step)
        copies.append(pltpu.make_async_copy(cot.at[:, cols], cot_here.at[:, cols], sems.at[j]))
        copies[-1].start()
    first.wait()
    total = None
    for j in range(count):
        cols = pl.ds(j * step, step)
        copies[j].wait()
        part = dot(up_here[:, cols], cot_here[:, cols], LAST_LAST)
        total = part if total is None else total + part
    back[...] = total


def low_kernel(rows, cols, acts, down, cot, grad_up, blocks):
    low = dot(down[...], acts[...], LAST_LAST).astype(jnp.bfloat16)
    grad_up[...] = dot(low, cot[...], LAST_FIRST)
    for s in range(blocks.shape[0]):
        r = pl.ds(pl.multiple_of(rows[0, s] * BLK, BLK), BLK)
        c = pl.ds(pl.multiple_of(cols[0, s] * BLK, BLK), BLK)
        blocks[s] = dot(acts[:, r], cot[:, c], FIRST_FIRST)


def down_kernel(back, acts, panel, out):
    width = out.shape[1]
    mine = pl.ds(pl.multiple_of(panel[0] * width, width), width)
    out[...] = dot(back[...].astype(jnp.bfloat16), acts[:, mine], LAST_FIRST)


def swap(x, axis, bit):
    return lax.ppermute(x, axis, [(i, i ^ bit) for i in range(lax.axis_size(axis))])


def body(acts, cot, down, up, rows, cols, live):
    tokens, width = acts.shape
    features = cot.shape[1]
    slots = rows.shape[1]
    dp, panels = lax.axis_size("dp"), lax.axis_size("panel")
    me = lax.axis_index("dp")
    own = slots // dp
    f32 = jnp.float32
    far = [1 << b for b in range(1, dp.bit_length() - 1)]
    wire = jnp.bfloat16 if len(far) == 1 else f32
    rank = down.shape[0]
    half = rank // 2
    core = me % 2

    hbm = functools.partial(pltpu.with_memory_space_constraint, memory_space=pltpu.HBM)
    vmem = functools.partial(pltpu.with_memory_space_constraint, memory_space=pltpu.VMEM)
    steps = max(1, features // COT_CHUNK)
    back, cot_here = call(
        back_kernel,
        (pltpu.VMEM((rank, tokens), f32), pltpu.VMEM((tokens, features), jnp.bfloat16)),
        [IN_HBM, IN_HBM],
        (hbm(cot), hbm(up)),
        [pltpu.VMEM((rank, features), jnp.bfloat16), pltpu.SemaphoreType.DMA((steps + 1,))],
        flops=2 * 256 * tokens * features,
        moved=2 * tokens * features,
    )
    acts_here = vmem(acts)
    grad_up, blocks = call(
        low_kernel,
        (pltpu.VMEM((rank, features), f32), pltpu.VMEM((slots, BLK, BLK), f32)),
        [IN_SMEM, IN_SMEM, IN_VMEM, IN_VMEM, IN_VMEM],
        (rows, cols, acts_here, down, cot_here),
        flops=2 * 256 * tokens * (features + width),
        moved=2 * tokens * width,
    )
    bit = 1
    while bit < panels:
        back = back + swap(back, "panel", bit)
        bit *= 2
    grad_down = call(
        down_kernel,
        pltpu.VMEM((rank, width // panels), f32),
        [IN_VMEM, IN_VMEM, IN_SMEM],
        (back, acts_here, lax.axis_index("panel").astype(jnp.int32)[None]),
        flops=2 * 256 * tokens * width // panels,
        moved=2 * tokens * width // panels,
    )

    def reduce_scatter_rows(x):
        mine = lax.dynamic_slice_in_dim(x, core * half, half, 0)
        other = lax.dynamic_slice_in_dim(x, (1 - core) * half, half, 0)
        return mine + swap(other, "dp", 1)

    def far_sum(x):
        for b in far:
            y = x.astype(wire)
            x = y.astype(f32) + swap(y, "dp", b).astype(f32)
        return x

    def gather_rows(x):
        other = swap(x, "dp", 1)
        both = jnp.where(core == 0, jnp.concatenate([x, other]), jnp.concatenate([other, x]))
        return both

    blocks = blocks.reshape(dp // 2, 2, own, BLK, BLK)
    pick = lambda x, i, axis: lax.dynamic_index_in_dim(x, i, axis, keepdims=False)
    blocks = pick(blocks, core, 1) + swap(pick(blocks, 1 - core, 1), "dp", 1)
    for b in reversed(far):
        count = blocks.shape[0] // 2
        split = blocks.reshape(2, count, own, BLK, BLK)
        side = (me // b) % 2
        sent = swap(pick(split, 1 - side, 0).astype(wire), "dp", b)
        blocks = pick(split, side, 0) + sent.astype(f32)
    blocks = blocks.reshape(own, BLK, BLK)
    alive = me * own + jnp.arange(own, dtype=jnp.int32) < live[0]
    blocks = jnp.where(alive[:, None, None], blocks, f32(0.0))[None]

    grad_up = gather_rows(far_sum(reduce_scatter_rows(grad_up)))
    grad_down = gather_rows(far_sum(reduce_scatter_rows(grad_down)))
    return blocks, grad_down, grad_up


def solution(mesh):
    in_specs = (
        P(("job", "dp"), None),
        P(("job", "dp"), "panel"),
        P("job", None),
        P("job", "panel"),
        P(("job", "panel"), None),
        P(("job", "panel"), None),
        P(("job", "panel")),
    )
    out_specs = (P(("job", "panel"), "dp", None, None), P("job", "panel"), P("job", "panel"))
    return jax.shard_map(body, mesh=mesh, in_specs=in_specs, out_specs=out_specs, check_vma=False)
```

time: 144 us -> 38.1 us (0.26)
  local copies, waits for them, and re-layouts: 45.3 us -> 6.84 us
  blocking collectives: 25.8 us -> 0 us
  matrix products: 22.2 us -> 0 us
  waiting for transfers between devices: 27 us -> 8.28 us
  between operations: 14.8 us -> 1.49 us
  Pallas kernels: 0 us -> 8.47 us
  starting transfers between devices: 4.21 us -> 10.5 us
    gather x48 -> x0, local copies, waits for them, and re-layouts: 37.1 us -> none
    psum x1 -> x0, waiting for transfers between devices: 27 us -> none  [body(): grad_down, grad_up = lax.psum((grad_down_part, grad_up_part), 'dp')]
    psum x1 -> x0, blocking collectives: 25.8 us -> none  [body(): backward_projection = lax.psum(back_part, 'panel').astype(jnp.bfloat16)]
    dot_general x4 -> x0, matrix products: 22.2 us -> none  [the longest x1 11.4 us: body(): lax.dot_general(lowrank_input, cotangent, contract_first, preferred_eleme...]
    ppermute x0 -> x10, starting transfers between devices: none -> 10.5 us  [swap(): lax.ppermute(x, axis, [(i, i ^ bit) for i in range(lax.axis_size(axis))])]
    pallas_call x0 -> x3, Pallas kernels: none -> 8.47 us  [call(): pl.pallas_call(kernel, out_shape=outs, in_specs=specs, out_specs=jax.tree...]
    ppermute x0 -> x10, waiting for transfers between devices: none -> 8.28 us  [swap(): lax.ppermute(x, axis, [(i, i ^ bit) for i in range(lax.axis_size(axis))])]
    all_to_all x1 -> x0, starting transfers between devices: 4.21 us -> none  [body(): lax.all_to_all(stacked, 'dp', split_axis=1, concat_axis=3, tiled=True)]
  transfers between devices with their start and end apart: 2 -> 10, of which waited for: 1 -> 4; matrix products, arithmetic and copies ran while one was open for 19% -> 4% of each run, Pallas kernels for 0% -> 13%
where the time goes in v1:
time: 38.1 us; the launch traced here: 37.9 us
  starting transfers between devices  10.5 us (28%)
  Pallas kernels  8.47 us (22%)
  waiting for transfers between devices  8.28 us (22%)
  local copies, waits for them, and re-layouts  6.84 us (18%)
  other arithmetic  2.33 us (6%)
  between operations  1.49 us (4%)
    ppermute x10, starting transfers between devices, swap(): lax.ppermute(x, axis, [(i, i ^ bit) for i in range(lax.axis_size(axis))])  10.5 us
    pallas_call x3, Pallas kernels, call(): pl.pallas_call(kernel, out_shape=outs, in_specs=specs, out_specs=jax.tree...  8.47 us
    ppermute x10, waiting for transfers between devices, swap(): lax.ppermute(x, axis, [(i, i ^ bit) for i in range(lax.axis_size(axis))])  8.28 us
    unnamed x10, local copies, waits for them, and re-layouts  6.77 us
    select_n x2, other arithmetic, gather_rows(): jnp.where(core == 0, jnp.concatenate([x, other]), jnp.concatenate([other,...  1.47 us
  transfers between devices with their start and end apart: 10, of which 4 were waited for; matrix products, arithmetic and copies ran while one was open for 4% of the time, Pallas kernels for 13%

profile of v1, /device:TPU:0, one launch (start us, length us, event | category | flops | bytes accessed | tf_op | source)
XLA Modules:
  0.0 37.9 jit_solution(11026890762764978042)
XLA Ops:
  0.6 0.0 copy-start.3
  0.6 0.0 copy-start.4
  0.7 0.0 copy-start.2
  0.7 3.7 %shard_map.94 = (f32[16,512]{1,0:T(8,128)S(1)}, bf16[512,7168]{1,0:T(8,128)(2,1)S(1)}) custom-call(bf16[512,7168]{1,0:T(8,128)(2,1)} %cot.1, bf16[16,7168]{1,0:T(8,128)(2,1)} %up.1), custom_call_target="tpu_custom_call" | custom-call | flops 1879048192 | bytes 7340032 | tf_op jit(solution)/shard_map/pallas_call | solution.py:26
  4.3 3.1 %collective-permute-start.2 = (f32[16,512]{1,0:T(8,128)S(1)}, f32[16,512]{1,0:T(8,128)S(1)}, u32[]{:S(2)}, u32[]{:S(2)}) collective-permute-start(f32[16,512]{1,0:T(8,128)S(1)} %get-tuple-element.9), channel_id=1, source_target_pairs={{0,1},{1,0},{2,3},{3,2},{4,5},{5,4},{6,7},{7,6},{8,9},{9,8},{10,11... | collective-permute-start | bytes 98312 | tf_op jit(solution)/shard_map/ppermute | solution.py:74
  7.4 0.0 copy-done.3
  7.4 0.0 copy-done.4
  7.4 0.0 copy-done.2
  7.4 0.0 copy-start
  7.4 3.4 %copy-done = bf16[512,8192]{1,0:T(8,128)(2,1)S(1)} copy-done((bf16[512,8192]{1,0:T(8,128)(2,1)S(1)}, bf16[512,8192]{1,0:T(8,128)(2,1)}, u32[]{:S(2)}) %copy-start) | copy-done | bytes 8388632
  10.8 4.4 %shard_map.95 = (f32[16,7168]{1,0:T(8,128)S(1)}, f32[8,128,128]{2,1,0:T(8,128)S(1)}) custom-call(s32[1,8]{1,0:T(1,128)S(1)} %copy-done.3, s32[1,8]{1,0:T(1,128)S(1)} %copy-done.4, bf16[512,8192]{1,0:T(8,128)(2,1)S(1)} %copy-done, bf16[16,8192]{1,0:T(8,128)(2,1)S(1)} %copy-done.2, bf16[512,7168]{1,0:T(8,128)(2,1)S(1)} %get-tuple-element.7.cot), custom_call_target="tpu_custom_call" | custom-call | flops 4026531840 | bytes 8388608 | tf_op jit(solution)/shard_map/pallas_call | solution.py:26
  15.3 0.0 collective-permute-done.2
  15.3 2.7 %collective-permute-start.3 = (f32[16,512]{1,0:T(8,128)S(1)}, f32[16,512]{1,0:T(8,128)S(1)}, u32[]{:S(2)}, u32[]{:S(2)}) collective-permute-start(f32[16,512]{1,0:T(8,128)S(1)} %add.76), channel_id=1, source_target_pairs={{0,2},{1,3},{2,0},{3,1},{4,6},{5,7},{6,4},{7,5},{8,10},{9,11},{10,... | collective-permute-start | bytes 98312 | tf_op jit(solution)/shard_map/ppermute | solution.py:74
  18.0 0.1 collective-permute-start
  18.1 2.1 %collective-permute-done.3 = f32[16,512]{1,0:T(8,128)S(1)} collective-permute-done((f32[16,512]{1,0:T(8,128)S(1)}, f32[16,512]{1,0:T(8,128)S(1)}, u32[]{:S(2)}, u32[]{:S(2)}) %collective-permute-start.3) | collective-permute-done | bytes 32800 | tf_op jit(solution)/shard_map/ppermute | solution.py:74
  20.2 0.0 copy-start.1
  20.2 3.4 %copy-done.1 = bf16[512,8192]{1,0:T(8,128)(2,1)S(1)} copy-done((bf16[512,8192]{1,0:T(8,128)(2,1)S(1)}, bf16[512,8192]{1,0:T(8,128)(2,1)}, u32[]{:S(2)}) %copy-start.1) | copy-done | bytes 8388632
  23.6 0.4 shard_map.96
  23.9 0.1 collective-permute-start.4
  24.0 0.5 %collective-permute-start.7 = (f32[8,7168]{1,0:T(8,128)S(1)}, f32[8,7168]{1,0:T(8,128)S(1)}, u32[]{:S(2)}, u32[]{:S(2)}) collective-permute-start(f32[8,7168]{1,0:T(8,128)S(1)} %constant_dynamic-slice_fusion), channel_id=1, source_target_pairs={{0,4},{4,0},{8,12},{12,8},{1,5},{5,1},{9,13},{13,9},{2,6},{6,2},{1... | collective-permute-start | bytes 688136 | tf_op jit(solution)/shard_map/ppermute | solution.py:74
  25.2 0.0 collective-permute-done.4
  25.3 1.8 %collective-permute-start.5 = (bf16[8,2048]{1,0:T(8,128)(2,1)S(1)}, bf16[8,2048]{1,0:T(8,128)(2,1)S(1)}, u32[]{:S(2)}, u32[]{:S(2)}) collective-permute-start(bf16[8,2048]{1,0:T(8,128)(2,1)S(1)} %add_convert_fusion.1), channel_id=1, source_target_pairs={{0,8},{4,12},{8,0},{12,4},{1,9},{5,13},{9,1},{13,5},{2,10},{6,14},... | collective-permute-start | bytes 98312 | tf_op jit(solution)/shard_map/ppermute | solution.py:74
  27.1 2.2 %collective-permute-done.5 = bf16[8,2048]{1,0:T(8,128)(2,1)S(1)} collective-permute-done((bf16[8,2048]{1,0:T(8,128)(2,1)S(1)}, bf16[8,2048]{1,0:T(8,128)(2,1)S(1)}, u32[]{:S(2)}, u32[]{:S(2)}) %collective-permute-start.5) | collective-permute-done | bytes 32800 | tf_op jit(solution)/shard_map/ppermute | solution.py:74
  29.3 0.1 collective-permute-start.6
  29.3 0.0 collective-permute-done.7
  29.4 1.8 %collective-permute-start.8 = (bf16[8,7168]{1,0:T(8,128)(2,1)S(1)}, bf16[8,7168]{1,0:T(8,128)(2,1)S(1)}, u32[]{:S(2)}, u32[]{:S(2)}) collective-permute-start(bf16[8,7168]{1,0:T(8,128)(2,1)S(1)} %add_convert_fusion), channel_id=1, source_target_pairs={{0,8},{4,12},{8,0},{12,4},{1,9},{5,13},{9,1},{13,5},{2,10},{6,14},... | collective-permute-start | bytes 344072 | tf_op jit(solution)/shard_map/ppermute | solution.py:74
  31.2 0.0 collective-permute-done
  31.2 0.4 collective-permute-start.1
  31.6 3.8 %collective-permute-done.8 = bf16[8,7168]{1,0:T(8,128)(2,1)S(1)} collective-permute-done((bf16[8,7168]{1,0:T(8,128)(2,1)S(1)}, bf16[8,7168]{1,0:T(8,128)(2,1)S(1)}, u32[]{:S(2)}, u32[]{:S(2)}) %collective-permute-start.8) | collective-permute-done | bytes 114720 | tf_op jit(solution)/shard_map/ppermute | solution.py:74
  35.4 0.1 collective-permute-start.9
  35.5 0.0 collective-permute-done.6
  35.5 0.7 %maximum_select_fusion.1 = f32[16,2048]{1,0:T(8,128)} fusion(f32[8,2048]{1,0:T(8,128)S(1)} %collective-permute-done.6, f32[8,2048]{1,0:T(8,128)S(1)} %convert_add_fusion.1, pred[]{:T(512)S(6)} %eq.7), kind=kLoop, calls=%fused_computation.5 | loop fusion | flops 98304 | bytes 262145 | tf_op jit(solution)/shard_map/jit(_where)/select_n | solution.py:138
  36.2 0.2 collective-permute-done.1
  36.4 0.7 %add_select_fusion = f32[1,2,128,128]{3,2,1,0:T(8,128)} fusion(bf16[1,2,128,128]{3,2,1,0:T(8,128)(2,1)S(1)} %collective-permute-done.1, f32[2,2,128,128]{3,2,1,0:T(8,128)S(1)} %bitcast_add_fusion, s32[]{:T(128)S(6)} %select_n.63, pred[2]{0:T(512)(128)(4,1)S(1)} %add_compare_fusion), kind=kLoop, calls=%fused_computation.6 | loop fusion | flops 98304 | bytes 327686 | tf_op jit(solution)/shard_map/jit(_where)/select_n | solution.py:152
  37.1 0.0 collective-permute-done.9
  37.1 0.8 %maximum_select_fusion = f32[16,7168]{1,0:T(8,128)} fusion(f32[8,7168]{1,0:T(8,128)S(1)} %collective-permute-done.9, f32[8,7168]{1,0:T(8,128)S(1)} %convert_add_fusion, pred[]{:T(512)S(6)} %eq.7), kind=kLoop, calls=%fused_computation | loop fusion | flops 344064 | bytes 917505 | tf_op jit(solution)/shard_map/jit(_where)/select_n | solution.py:138
  (12 shorter events, 0.2 us)
Async XLA Ops:
  0.6 6.8 %copy-start.3 = (s32[1,8]{1,0:T(1,128)S(1)}, s32[1,8]{1,0:T(1,128)}, u32[]{:S(2)}) copy-start(s32[1,8]{1,0:T(1,128)} %rows.1) | copy-start | bytes 100
  0.6 6.8 %copy-start.4 = (s32[1,8]{1,0:T(1,128)S(1)}, s32[1,8]{1,0:T(1,128)}, u32[]{:S(2)}) copy-start(s32[1,8]{1,0:T(1,128)} %cols.1) | copy-start | bytes 100
  0.7 6.8 %copy-start.2 = (bf16[16,8192]{1,0:T(8,128)(2,1)S(1)}, bf16[16,8192]{1,0:T(8,128)(2,1)}, u32[]{:S(2)}) copy-start(bf16[16,8192]{1,0:T(8,128)(2,1)} %down.1) | copy-start | bytes 786436
  4.3 10.9 %collective-permute-start.2 = (f32[16,512]{1,0:T(8,128)S(1)}, f32[16,512]{1,0:T(8,128)S(1)}, u32[]{:S(2)}, u32[]{:S(2)}) collective-permute-start(f32[16,512]{1,0:T(8,128)S(1)} %get-tuple-element.9), channel_id=1, source_target_pairs={{0,1},{1,0},{2,3},{3,2},{4,5},{5,4},{6,7},{7,6},{8,9},{9,8},{10,11... | collective-permute-start | bytes 98312 | tf_op jit(solution)/shard_map/ppermute | solution.py:74
  7.4 3.4 %copy-start = (bf16[512,8192]{1,0:T(8,128)(2,1)S(1)}, bf16[512,8192]{1,0:T(8,128)(2,1)}, u32[]{:S(2)}) copy-start(bf16[512,8192]{1,0:T(8,128)(2,1)} %acts.3) | copy-start | bytes 25165828
  15.3 4.9 %collective-permute-start.3 = (f32[16,512]{1,0:T(8,128)S(1)}, f32[16,512]{1,0:T(8,128)S(1)}, u32[]{:S(2)}, u32[]{:S(2)}) collective-permute-start(f32[16,512]{1,0:T(8,128)S(1)} %add.76), channel_id=1, source_target_pairs={{0,2},{1,3},{2,0},{3,1},{4,6},{5,7},{6,4},{7,5},{8,10},{9,11},{10,... | collective-permute-start | bytes 98312 | tf_op jit(solution)/shard_map/ppermute | solution.py:74
  18.0 13.2 %collective-permute-start = (f32[2,2,128,128]{3,2,1,0:T(8,128)S(1)}, f32[2,2,128,128]{3,2,1,0:T(8,128)S(1)}, u32[]{:S(2)}, u32[]{:S(2)}) collective-permute-start(f32[2,2,128,128]{3,2,1,0:T(8,128)S(1)} %dynamic-slice_bitcast_fusion), channel_id=1, source_target_pairs={{0,4},{4,0},{8,12},{12,8},{1,5},{5,1},{9,13},{13,9},{2,6},{6,2},{1... | collective-permute-start | bytes 786440 | tf_op jit(solution)/shard_map/ppermute | solution.py:74
  20.2 3.4 %copy-start.1 = (bf16[512,8192]{1,0:T(8,128)(2,1)S(1)}, bf16[512,8192]{1,0:T(8,128)(2,1)}, u32[]{:S(2)}) copy-start(bf16[512,8192]{1,0:T(8,128)(2,1)} %acts.3) | copy-start | bytes 25165828
  23.9 1.3 %collective-permute-start.4 = (f32[8,2048]{1,0:T(8,128)S(1)}, f32[8,2048]{1,0:T(8,128)S(1)}, u32[]{:S(2)}, u32[]{:S(2)}) collective-permute-start(f32[8,2048]{1,0:T(8,128)S(1)} %constant_dynamic-slice_fusion.1), channel_id=1, source_target_pairs={{0,4},{4,0},{8,12},{12,8},{1,5},{5,1},{9,13},{13,9},{2,6},{6,2},{1... | collective-permute-start | bytes 196616 | tf_op jit(solution)/shard_map/ppermute | solution.py:74
  24.0 5.3 %collective-permute-start.7 = (f32[8,7168]{1,0:T(8,128)S(1)}, f32[8,7168]{1,0:T(8,128)S(1)}, u32[]{:S(2)}, u32[]{:S(2)}) collective-permute-start(f32[8,7168]{1,0:T(8,128)S(1)} %constant_dynamic-slice_fusion), channel_id=1, source_target_pairs={{0,4},{4,0},{8,12},{12,8},{1,5},{5,1},{9,13},{13,9},{2,6},{6,2},{1... | collective-permute-start | bytes 688136 | tf_op jit(solution)/shard_map/ppermute | solution.py:74
  25.3 4.0 %collective-permute-start.5 = (bf16[8,2048]{1,0:T(8,128)(2,1)S(1)}, bf16[8,2048]{1,0:T(8,128)(2,1)S(1)}, u32[]{:S(2)}, u32[]{:S(2)}) collective-permute-start(bf16[8,2048]{1,0:T(8,128)(2,1)S(1)} %add_convert_fusion.1), channel_id=1, source_target_pairs={{0,8},{4,12},{8,0},{12,4},{1,9},{5,13},{9,1},{13,5},{2,10},{6,14},... | collective-permute-start | bytes 98312 | tf_op jit(solution)/shard_map/ppermute | solution.py:74
  29.3 6.3 %collective-permute-start.6 = (f32[8,2048]{1,0:T(8,128)S(1)}, f32[8,2048]{1,0:T(8,128)S(1)}, u32[]{:S(2)}, u32[]{:S(2)}) collective-permute-start(f32[8,2048]{1,0:T(8,128)S(1)} %convert_add_fusion.1), channel_id=1, source_target_pairs={{0,4},{4,0},{8,12},{12,8},{1,5},{5,1},{9,13},{13,9},{2,6},{6,2},{1... | collective-permute-start | bytes 196616 | tf_op jit(solution)/shard_map/ppermute | solution.py:74
  29.4 6.0 %collective-permute-start.8 = (bf16[8,7168]{1,0:T(8,128)(2,1)S(1)}, bf16[8,7168]{1,0:T(8,128)(2,1)S(1)}, u32[]{:S(2)}, u32[]{:S(2)}) collective-permute-start(bf16[8,7168]{1,0:T(8,128)(2,1)S(1)} %add_convert_fusion), channel_id=1, source_target_pairs={{0,8},{4,12},{8,0},{12,4},{1,9},{5,13},{9,1},{13,5},{2,10},{6,14},... | collective-permute-start | bytes 344072 | tf_op jit(solution)/shard_map/ppermute | solution.py:74
  31.2 5.1 %collective-permute-start.1 = (bf16[1,2,128,128]{3,2,1,0:T(8,128)(2,1)S(1)}, bf16[1,2,128,128]{3,2,1,0:T(8,128)(2,1)S(1)}, u32[]{:S(2)}, u32[]{:S(2)}) collective-permute-start(bf16[1,2,128,128]{3,2,1,0:T(8,128)(2,1)S(1)} %dynamic-slice_convert_fusion), channel_id=1, source_target_pairs={{0,8},{4,12},{8,0},{12,4},{1,9},{5,13},{9,1},{13,5},{2,10},{6,14},... | collective-permute-start | bytes 196616 | tf_op jit(solution)/shard_map/ppermute | solution.py:74
  35.4 1.7 %collective-permute-start.9 = (f32[8,7168]{1,0:T(8,128)S(1)}, f32[8,7168]{1,0:T(8,128)S(1)}, u32[]{:S(2)}, u32[]{:S(2)}) collective-permute-start(f32[8,7168]{1,0:T(8,128)S(1)} %convert_add_fusion), channel_id=1, source_target_pairs={{0,4},{4,0},{8,12},{12,8},{1,5},{5,1},{9,13},{13,9},{2,6},{6,2},{1... | collective-permute-start | bytes 688136 | tf_op jit(solution)/shard_map/ppermute | solution.py:74

commit v2 on v0

v2 whole, which is shorter than its diff:
```python
import functools
import itertools

import jax
import jax.numpy as jnp
from jax import lax
from jax.experimental import pallas as pl
from jax.experimental.pallas import tpu as pltpu
from jax.sharding import PartitionSpec as P

BLK = 128
COT_CHUNK = 1024
AHEAD = 5
RADIX = 4
CROSS = 1
ACT_CHUNK = 1024
LAST_LAST = (((1,), (1,)), ((), ()))
LAST_FIRST = (((1,), (0,)), ((), ()))
FIRST_FIRST = (((0,), (0,)), ((), ()))
IN_HBM = pl.BlockSpec(memory_space=pltpu.HBM)
IN_VMEM = pl.BlockSpec(memory_space=pltpu.VMEM)


def dot(a, b, dims):
    return lax.dot_general(a, b, dims, preferred_element_type=jnp.float32)


def call(kernel, outs, specs, args, scratch=(), vmem=16, flops=0, moved=0):
    return pl.pallas_call(
        kernel,
        out_shape=outs,
        in_specs=specs,
        out_specs=jax.tree.map(lambda _: IN_VMEM, outs),
        scratch_shapes=scratch,
        cost_estimate=pl.CostEstimate(flops=flops, bytes_accessed=moved, transcendentals=0),
        compiler_params=pltpu.CompilerParams(vmem_limit_bytes=vmem * 2**20),
    )(*args)


def local_kernel(rows_hbm, cols_hbm, acts, cot, down, up, up_mine, up_other, blocks_mine, blocks_other, back,
                 acts_mine, rows, cols, acts_here, cot_here, down_here, up_here, act_sems, cot_sems, sems):
    core = lax.rem(lax.axis_index("dp"), 2)
    width, features, mine = acts.shape[1], cot.shape[1], acts_mine.shape[1]
    act_step, cot_step = min(ACT_CHUNK, width), min(COT_CHUNK, features)

    def stream(source, target, step, sem):
        chunks = [pl.ds(j * step, step) for j in range(source.shape[1] // step)]
        return [pltpu.make_async_copy(source.at[:, at], target.at[:, at], sem.at[j]) for j, at in enumerate(chunks)]

    factors = [
        pltpu.make_async_copy(down, down_here, sems.at[0]),
        pltpu.make_async_copy(up, up_here, sems.at[1]),
        pltpu.make_async_copy(rows_hbm, rows, sems.at[3]),
        pltpu.make_async_copy(cols_hbm, cols, sems.at[4]),
    ]
    act_copies = stream(acts, acts_here, act_step, act_sems)
    cot_copies = stream(cot, cot_here, cot_step, cot_sems)
    order = factors + act_copies + cot_copies
    for copy in order[: AHEAD + len(factors)]:
        copy.start()
    waiting = iter(order[AHEAD + len(factors) :])

    def arrive(copy):
        copy.wait()
        for later in itertools.islice(waiting, 1):
            later.start()

    for copy in factors:
        copy.wait()
    low = None
    for j, copy in enumerate(act_copies):
        arrive(copy)
        at = pl.ds(j * act_step, act_step)
        part = dot(down_here[:, at], acts_here[:, at], LAST_LAST)
        low = part if low is None else low + part
    low = low.astype(jnp.bfloat16)
    slice_at = pl.ds(pl.multiple_of(lax.axis_index("panel") * mine, mine), mine)
    keep = pltpu.make_async_copy(acts_here.at[:, slice_at], acts_mine, sems.at[2])
    keep.start()
    total = None
    for j, copy in enumerate(cot_copies):
        arrive(copy)
        at = pl.ds(j * cot_step, cot_step)
        part = dot(up_here[:, at], cot_here[:, at], LAST_LAST)
        total = part if total is None else total + part
        part = dot(low, cot_here[:, at], LAST_FIRST)
        first, second = part[: part.shape[0] // 2], part[part.shape[0] // 2 :]
        up_mine[:, at] = jnp.where(core == 0, first, second)
        up_other[:, at] = jnp.where(core == 0, second, first)
    back[...] = total
    chips, own = blocks_mine.shape[:2]
    for out, owner in ((blocks_other, 1 - core), (blocks_mine, core)):
        for chip in range(chips):
            for k in range(own):
                s = (2 * chip + owner) * own + k
                r = pl.ds(pl.multiple_of(rows[0, s] * BLK, BLK), BLK)
                c = pl.ds(pl.multiple_of(cols[0, s] * BLK, BLK), BLK)
                out[chip, k] = dot(acts_here[:, r], cot_here[:, c], FIRST_FIRST)
    keep.wait()


def down_kernel(*refs):
    *shares, acts, out = refs
    back = shares[0][...]
    for share in shares[1:]:
        back = back + share[...]
    out[...] = dot(back.astype(jnp.bfloat16), acts[...], LAST_FIRST)


def swap(x, axis, bits):
    return lax.ppermute(x, axis, [(i, i ^ bits) for i in range(lax.axis_size(axis))])


def body(acts, cot, down, up, rows, cols, live):
    tokens, width = acts.shape
    features = cot.shape[1]
    slots = rows.shape[1]
    rank = down.shape[0]
    dp, panels = lax.axis_size("dp"), lax.axis_size("panel")
    me = lax.axis_index("dp")
    core, own, mine = me % 2, slots // dp, width // panels
    f32, bf16 = jnp.float32, jnp.bfloat16
    far = [1 << b for b in range(1, dp.bit_length() - 1)]
    wire = bf16 if len(far) == 1 else f32

    hbm = functools.partial(pltpu.with_memory_space_constraint, memory_space=pltpu.HBM)
    half = rank // 2
    up_sum, up_other, blocks, blocks_other, back, acts_mine = call(
        local_kernel,
        (
            pltpu.VMEM((half, features), f32),
            pltpu.VMEM((half, features), f32),
            pltpu.VMEM((dp // 2, own, BLK, BLK), f32),
            pltpu.VMEM((dp // 2, own, BLK, BLK), f32),
            pltpu.VMEM((rank, tokens), f32),
            pltpu.VMEM((tokens, mine), bf16),
        ),
        [IN_HBM] * 6,
        (hbm(rows), hbm(cols), hbm(acts), hbm(cot), hbm(down), hbm(up)),
        [
            pltpu.SMEM((1, slots), jnp.int32),
            pltpu.SMEM((1, slots), jnp.int32),
            pltpu.VMEM((tokens, width), bf16),
            pltpu.VMEM((tokens, features), bf16),
            pltpu.VMEM((rank, width), bf16),
            pltpu.VMEM((rank, features), bf16),
            pltpu.SemaphoreType.DMA((width // min(ACT_CHUNK, width),)),
            pltpu.SemaphoreType.DMA((features // min(COT_CHUNK, features),)),
            pltpu.SemaphoreType.DMA((5,)),
        ],
        vmem=24,
        flops=2 * 256 * tokens * (2 * features + width),
        moved=2 * tokens * (features + width),
    )

    pick = lambda x, i, axis: lax.dynamic_index_in_dim(x, i, axis, keepdims=False)
    gu = up_sum + swap(up_other, "dp", 1)
    for b in far:
        sent = gu.astype(wire)
        gu = sent.astype(f32) + swap(sent, "dp", b).astype(f32)
    other = swap(gu, "dp", 1)
    grad_up = jnp.where(core == 0, jnp.concatenate([gu, other]), jnp.concatenate([other, gu]))

    blocks = blocks + swap(blocks_other, "dp", 1)
    for b in reversed(far):
        split = blocks.reshape(2, blocks.shape[0] // 2, own, BLK, BLK)
        side = (me // b) % 2
        sent = swap(pick(split, 1 - side, 0).astype(wire), "dp", b)
        blocks = pick(split, side, 0) + sent.astype(f32)
    blocks = blocks.reshape(own, BLK, BLK)
    alive = me * own + jnp.arange(own, dtype=jnp.int32) < live[0]
    blocks = jnp.where(alive[:, None, None], blocks, f32(0.0))[None]

    bit, shares = 1, [back]
    while bit < panels:
        base = functools.reduce(jnp.add, shares)
        radix = min(RADIX, panels // bit)
        shares = [base] + [swap(base, "panel", k * bit) for k in range(1, radix)]
        bit *= radix
    gd = call(
        down_kernel,
        pltpu.VMEM((rank, mine), f32),
        [IN_VMEM] * (len(shares) + 1),
        (*shares, acts_mine),
        flops=2 * 256 * tokens * mine,
        moved=2 * tokens * mine,
    )
    gd = gd + swap(gd, "dp", 1)
    for b in far:
        sent = gd.astype(wire)
        gd = sent.astype(f32) + swap(sent, "dp", b ^ CROSS).astype(f32)
    return blocks, gd, grad_up


def solution(mesh):
    in_specs = (
        P(("job", "dp"), None),
        P(("job", "dp"), "panel"),
        P("job", None),
        P("job", "panel"),
        P(("job", "panel"), None),
        P(("job", "panel"), None),
        P(("job", "panel")),
    )
    out_specs = (P(("job", "panel"), "dp", None, None), P("job", "panel"), P("job", "panel"))
    return jax.shard_map(body, mesh=mesh, in_specs=in_specs, out_specs=out_specs, check_vma=False)
```

time: 144 us -> 31 us (0.22)
  local copies, waits for them, and re-layouts: 45.3 us -> 0.02 us
  blocking collectives: 25.8 us -> 0 us
  matrix products: 22.2 us -> 0 us
  waiting for transfers between devices: 27 us -> 7.5 us
  between operations: 14.8 us -> 1.38 us
  Pallas kernels: 0 us -> 9.21 us
  starting transfers between devices: 4.21 us -> 9.45 us
    gather x48 -> x0, local copies, waits for them, and re-layouts: 37.1 us -> none
    psum x1 -> x0, waiting for transfers between devices: 27 us -> none  [body(): grad_down, grad_up = lax.psum((grad_down_part, grad_up_part), 'dp')]
    psum x1 -> x0, blocking collectives: 25.8 us -> none  [body(): backward_projection = lax.psum(back_part, 'panel').astype(jnp.bfloat16)]
    dot_general x4 -> x0, matrix products: 22.2 us -> none  [the longest x1 11.4 us: body(): lax.dot_general(lowrank_input, cotangent, contract_first, preferred_eleme...]
    ppermute x0 -> x10, starting transfers between devices: none -> 9.45 us  [swap(): lax.ppermute(x, axis, [(i, i ^ bits) for i in range(lax.axis_size(axis))])]
    pallas_call x0 -> x2, Pallas kernels: none -> 9.21 us  [call(): pl.pallas_call(kernel, out_shape=outs, in_specs=specs, out_specs=jax.tree...]
    ppermute x0 -> x10, waiting for transfers between devices: none -> 7.5 us  [swap(): lax.ppermute(x, axis, [(i, i ^ bits) for i in range(lax.axis_size(axis))])]
    all_to_all x1 -> x0, starting transfers between devices: 4.21 us -> none  [body(): lax.all_to_all(stacked, 'dp', split_axis=1, concat_axis=3, tiled=True)]
  transfers between devices with their start and end apart: 2 -> 10, of which waited for: 1 -> 5; matrix products, arithmetic and copies ran while one was open for 19% -> 8% of each run, Pallas kernels for 0% -> 1%
where the time goes in v2:
time: 31 us; the launch traced here: 30.8 us
  starting transfers between devices  9.45 us (30%)
  Pallas kernels  9.21 us (30%)
  waiting for transfers between devices  7.5 us (24%)
  other arithmetic  3.26 us (11%)
  between operations  1.38 us (4%)
    ppermute x10, starting transfers between devices, swap(): lax.ppermute(x, axis, [(i, i ^ bits) for i in range(lax.axis_size(axis))])  9.45 us
    pallas_call x2, Pallas kernels, call(): pl.pallas_call(kernel, out_shape=outs, in_specs=specs, out_specs=jax.tree...  9.21 us
    ppermute x10, waiting for transfers between devices, swap(): lax.ppermute(x, axis, [(i, i ^ bits) for i in range(lax.axis_size(axis))])  7.5 us
    convert_element_type x1, other arithmetic, body(): sent = gu.astype(wire)  0.98 us
    select_n x1, other arithmetic, body(): jnp.where(core == 0, jnp.concatenate([gu, other]), jnp.concatenate([other...  0.8 us
    select_n x1, other arithmetic, body(): blocks = jnp.where(alive[:, None, None], blocks, f32(0.0))[None]  0.73 us
    add x1, other arithmetic, body(): gd = sent.astype(f32) + swap(sent, 'dp', b ^ CROSS).astype(f32)  0.67 us
  transfers between devices with their start and end apart: 10, of which 5 were waited for; matrix products, arithmetic and copies ran while one was open for 8% of the time, Pallas kernels for 1%

profile of v2, /device:TPU:0, one launch (start us, length us, event | category | flops | bytes accessed | tf_op | source)
XLA Modules:
  0.0 30.8 jit_solution(9067066048743379012)
XLA Ops:
  0.6 8.8 %shard_map.94 = (f32[8,7168]{1,0:T(8,128)S(1)}, f32[8,7168]{1,0:T(8,128)S(1)}, f32[2,2,128,128]{3,2,1,0:T(8,128)S(1)}, f32[2,2,128,128]{3,2,1,0:T(8,128)S(1)}, f...) custom-call(s32[1,8]{1,0:T(1,128)} %rows_hbm.1, s32[1,8]{1,0:T(1,128)} %cols_hbm.1, bf16[512,8192]{1,0:T(8,128)(2,1)} %acts.1, ...), custom_call_target="tpu_custom_call" | custom-call | flops 5905580032 | bytes 15728640 | tf_op jit(solution)/shard_map/pallas_call | solution.py:29
  9.5 0.5 %collective-permute-start.7 = (f32[8,7168]{1,0:T(8,128)S(1)}, f32[8,7168]{1,0:T(8,128)}, u32[]{:S(2)}, u32[]{:S(2)}) collective-permute-start(f32[8,7168]{1,0:T(8,128)S(1)} %get-tuple-element.14), channel_id=1, source_target_pairs={{0,4},{4,0},{8,12},{12,8},{1,5},{5,1},{9,13},{13,9},{2,6},{6,2},{1... | collective-permute-start | bytes 688136 | tf_op jit(solution)/shard_map/ppermute | solution.py:111
  10.0 4.7 %collective-permute-start.4 = (f32[16,512]{1,0:T(8,128)S(1)}, f32[16,512]{1,0:T(8,128)S(1)}, u32[]{:S(2)}, u32[]{:S(2)}) collective-permute-start(f32[16,512]{1,0:T(8,128)S(1)} %get-tuple-element.11.refs_0_), channel_id=1, source_target_pairs={{0,3},{1,2},{2,1},{3,0},{4,7},{5,6},{6,5},{7,4},{8,11},{9,10},{10,... | collective-permute-start | bytes 98312 | tf_op jit(solution)/shard_map/ppermute | solution.py:111
  14.7 0.0 collective-permute-start.3
  14.7 0.6 %collective-permute-start.2 = (f32[16,512]{1,0:T(8,128)S(1)}, f32[16,512]{1,0:T(8,128)S(1)}, u32[]{:S(2)}, u32[]{:S(2)}) collective-permute-start(f32[16,512]{1,0:T(8,128)S(1)} %get-tuple-element.11.refs_0_), channel_id=1, source_target_pairs={{0,1},{1,0},{2,3},{3,2},{4,5},{5,4},{6,7},{7,6},{8,9},{9,8},{10,11... | collective-permute-start | bytes 98312 | tf_op jit(solution)/shard_map/ppermute | solution.py:111
  15.3 0.0 collective-permute-start
  16.0 0.7 %collective-permute-done.4.refs_3_ = f32[16,512]{1,0:T(8,128)S(1)} collective-permute-done((f32[16,512]{1,0:T(8,128)S(1)}, f32[16,512]{1,0:T(8,128)S(1)}, u32[]{:S(2)}, u32[]{:S(2)}) %collective-permute-start.4) | collective-permute-done | bytes 32800 | tf_op jit(solution)/shard_map/ppermute | solution.py:111
  16.7 2.8 %collective-permute-done.3.refs_2_ = f32[16,512]{1,0:T(8,128)S(1)} collective-permute-done((f32[16,512]{1,0:T(8,128)S(1)}, f32[16,512]{1,0:T(8,128)S(1)}, u32[]{:S(2)}, u32[]{:S(2)}) %collective-permute-start.3) | collective-permute-done | bytes 32800 | tf_op jit(solution)/shard_map/ppermute | solution.py:111
  19.5 0.0 collective-permute-done.2.refs_1_
  19.5 0.4 %shard_map.95 = f32[16,2048]{1,0:T(8,128)S(1)} custom-call(f32[16,512]{1,0:T(8,128)S(1)} %get-tuple-element.11.refs_0_, f32[16,512]{1,0:T(8,128)S(1)} %collective-permute-done.2.refs_1_, f32[16,512]{1,0:T(8,128)S(1)} %collective-permute-done.3.refs_2_, f32[16,512]{1,0:T(8,128)S(1)} %collective-permute-done.4.refs_3_, ...), custom_call_target="tpu_custom_call" | custom-call | flops 536870912 | bytes 2097152 | tf_op jit(solution)/shard_map/pallas_call | solution.py:29
  19.9 0.0 collective-permute-start.5
  19.9 0.0 collective-permute-done.7
  19.9 1.0 %add_convert_fusion = bf16[8,7168]{1,0:T(8,128)(2,1)S(1)} fusion(f32[8,7168]{1,0:T(8,128)S(1)} %get-tuple-element.13, f32[8,7168]{1,0:T(8,128)} %collective-permute-done.7), kind=kLoop, calls=%fused_computation.2 | loop fusion | flops 114688 | bytes 573440 | tf_op jit(solution)/shard_map/convert_element_type | solution.py:159
  20.9 1.5 %collective-permute-start.8 = (bf16[8,7168]{1,0:T(8,128)(2,1)S(1)}, bf16[8,7168]{1,0:T(8,128)(2,1)S(1)}, u32[]{:S(2)}, u32[]{:S(2)}) collective-permute-start(bf16[8,7168]{1,0:T(8,128)(2,1)S(1)} %add_convert_fusion), channel_id=1, source_target_pairs={{0,8},{4,12},{8,0},{12,4},{1,9},{5,13},{9,1},{13,5},{2,10},{6,14},... | collective-permute-start | bytes 344072 | tf_op jit(solution)/shard_map/ppermute | solution.py:111
  22.4 0.0 collective-permute-done.5
  22.4 0.4 %collective-permute-start.6 = (bf16[16,2048]{1,0:T(8,128)(2,1)S(1)}, bf16[16,2048]{1,0:T(8,128)(2,1)S(1)}, u32[]{:S(2)}, u32[]{:S(2)}) collective-permute-start(bf16[16,2048]{1,0:T(8,128)(2,1)S(1)} %add_convert_fusion.1), channel_id=1, source_target_pairs={{0,12},{4,8},{8,4},{12,0},{1,13},{5,9},{9,5},{13,1},{2,14},{6,10},... | collective-permute-start | bytes 196616 | tf_op jit(solution)/shard_map/ppermute | solution.py:111
  22.9 0.0 collective-permute-done
  22.9 1.5 %collective-permute-start.1 = (bf16[1,2,128,128]{3,2,1,0:T(8,128)(2,1)S(1)}, bf16[1,2,128,128]{3,2,1,0:T(8,128)(2,1)S(1)}, u32[]{:S(2)}, u32[]{:S(2)}) collective-permute-start(bf16[1,2,128,128]{3,2,1,0:T(8,128)(2,1)S(1)} %dynamic-slice_convert_fusion), channel_id=1, source_target_pairs={{0,8},{4,12},{8,0},{12,4},{1,9},{5,13},{9,1},{13,5},{2,10},{6,14},... | collective-permute-start | bytes 196616 | tf_op jit(solution)/shard_map/ppermute | solution.py:111
  24.5 2.4 %collective-permute-done.8 = bf16[8,7168]{1,0:T(8,128)(2,1)S(1)} collective-permute-done((bf16[8,7168]{1,0:T(8,128)(2,1)S(1)}, bf16[8,7168]{1,0:T(8,128)(2,1)S(1)}, u32[]{:S(2)}, u32[]{:S(2)}) %collective-permute-start.8) | collective-permute-done | bytes 114720 | tf_op jit(solution)/shard_map/ppermute | solution.py:111
  26.9 0.1 collective-permute-start.9
  27.0 0.5 %collective-permute-done.6 = bf16[16,2048]{1,0:T(8,128)(2,1)S(1)} collective-permute-done((bf16[16,2048]{1,0:T(8,128)(2,1)S(1)}, bf16[16,2048]{1,0:T(8,128)(2,1)S(1)}, u32[]{:S(2)}, u32[]{:S(2)}) %collective-permute-start.6) | collective-permute-done | bytes 65568 | tf_op jit(solution)/shard_map/ppermute | solution.py:111
  27.5 0.7 %convert_add_fusion.1 = f32[16,2048]{1,0:T(8,128)} fusion(bf16[16,2048]{1,0:T(8,128)(2,1)S(1)} %collective-permute-done.6, bf16[16,2048]{1,0:T(8,128)(2,1)S(1)} %add_convert_fusion.1), kind=kLoop, calls=%fused_computation.3 | loop fusion | flops 98304 | bytes 262144 | tf_op jit(solution)/shard_map/add | solution.py:191
  28.2 1.1 %collective-permute-done.1 = bf16[1,2,128,128]{3,2,1,0:T(8,128)(2,1)S(1)} collective-permute-done((bf16[1,2,128,128]{3,2,1,0:T(8,128)(2,1)S(1)}, bf16[1,2,128,128]{3,2,1,0:T(8,128)(2,1)S(1)}, u32[]{:S(2)}, u32[]{:S(2)}) %collective-permute-start.1) | collective-permute-done | bytes 65568 | tf_op jit(solution)/shard_map/ppermute | solution.py:111
  29.3 0.7 %add_select_fusion = f32[1,2,128,128]{3,2,1,0:T(8,128)} fusion(bf16[1,2,128,128]{3,2,1,0:T(8,128)(2,1)S(1)} %collective-permute-done.1, f32[2,2,128,128]{3,2,1,0:T(8,128)S(1)} %add.46, s32[]{:T(128)S(6)} %select_n.37, pred[2]{0:T(512)(128)(4,1)S(1)} %add_compare_fusion), kind=kLoop, calls=%fused_computation.5 | loop fusion | flops 98304 | bytes 327686 | tf_op jit(solution)/shard_map/jit(_where)/select_n | solution.py:172
  30.0 0.0 collective-permute-done.9
  30.0 0.8 %maximum_select_fusion = f32[16,7168]{1,0:T(8,128)} fusion(f32[8,7168]{1,0:T(8,128)S(1)} %collective-permute-done.9, f32[8,7168]{1,0:T(8,128)S(1)} %convert_add_fusion, pred[]{:T(512)S(6)} %eq.6), kind=kLoop, calls=%fused_computation | loop fusion | flops 344064 | bytes 917505 | tf_op jit(solution)/shard_map/jit(_where)/select_n | solution.py:162
  (5 shorter events, 0.1 us)
Async XLA Ops:
  9.5 10.4 %collective-permute-start.7 = (f32[8,7168]{1,0:T(8,128)S(1)}, f32[8,7168]{1,0:T(8,128)}, u32[]{:S(2)}, u32[]{:S(2)}) collective-permute-start(f32[8,7168]{1,0:T(8,128)S(1)} %get-tuple-element.14), channel_id=1, source_target_pairs={{0,4},{4,0},{8,12},{12,8},{1,5},{5,1},{9,13},{13,9},{2,6},{6,2},{1... | collective-permute-start | bytes 688136 | tf_op jit(solution)/shard_map/ppermute | solution.py:111
  10.0 6.7 %collective-permute-start.4 = (f32[16,512]{1,0:T(8,128)S(1)}, f32[16,512]{1,0:T(8,128)S(1)}, u32[]{:S(2)}, u32[]{:S(2)}) collective-permute-start(f32[16,512]{1,0:T(8,128)S(1)} %get-tuple-element.11.refs_0_), channel_id=1, source_target_pairs={{0,3},{1,2},{2,1},{3,0},{4,7},{5,6},{6,5},{7,4},{8,11},{9,10},{10,... | collective-permute-start | bytes 98312 | tf_op jit(solution)/shard_map/ppermute | solution.py:111
  14.7 4.8 %collective-permute-start.3 = (f32[16,512]{1,0:T(8,128)S(1)}, f32[16,512]{1,0:T(8,128)S(1)}, u32[]{:S(2)}, u32[]{:S(2)}) collective-permute-start(f32[16,512]{1,0:T(8,128)S(1)} %get-tuple-element.11.refs_0_), channel_id=1, source_target_pairs={{0,2},{1,3},{2,0},{3,1},{4,6},{5,7},{6,4},{7,5},{8,10},{9,11},{10,... | collective-permute-start | bytes 98312 | tf_op jit(solution)/shard_map/ppermute | solution.py:111
  14.7 4.8 %collective-permute-start.2 = (f32[16,512]{1,0:T(8,128)S(1)}, f32[16,512]{1,0:T(8,128)S(1)}, u32[]{:S(2)}, u32[]{:S(2)}) collective-permute-start(f32[16,512]{1,0:T(8,128)S(1)} %get-tuple-element.11.refs_0_), channel_id=1, source_target_pairs={{0,1},{1,0},{2,3},{3,2},{4,5},{5,4},{6,7},{7,6},{8,9},{9,8},{10,11... | collective-permute-start | bytes 98312 | tf_op jit(solution)/shard_map/ppermute | solution.py:111
  15.3 7.5 %collective-permute-start = (f32[2,2,128,128]{3,2,1,0:T(8,128)S(1)}, f32[2,2,128,128]{3,2,1,0:T(8,128)S(1)}, u32[]{:S(2)}, u32[]{:S(2)}) collective-permute-start(f32[2,2,128,128]{3,2,1,0:T(8,128)S(1)} %get-tuple-element.10), channel_id=1, source_target_pairs={{0,4},{4,0},{8,12},{12,8},{1,5},{5,1},{9,13},{13,9},{2,6},{6,2},{1... | collective-permute-start | bytes 786440 | tf_op jit(solution)/shard_map/ppermute | solution.py:111
  19.9 2.5 %collective-permute-start.5 = (f32[16,2048]{1,0:T(8,128)S(1)}, f32[16,2048]{1,0:T(8,128)S(1)}, u32[]{:S(2)}, u32[]{:S(2)}) collective-permute-start(f32[16,2048]{1,0:T(8,128)S(1)} %shard_map.95), channel_id=1, source_target_pairs={{0,4},{4,0},{8,12},{12,8},{1,5},{5,1},{9,13},{13,9},{2,6},{6,2},{1... | collective-permute-start | bytes 393224 | tf_op jit(solution)/shard_map/ppermute | solution.py:111
  20.9 6.0 %collective-permute-start.8 = (bf16[8,7168]{1,0:T(8,128)(2,1)S(1)}, bf16[8,7168]{1,0:T(8,128)(2,1)S(1)}, u32[]{:S(2)}, u32[]{:S(2)}) collective-permute-start(bf16[8,7168]{1,0:T(8,128)(2,1)S(1)} %add_convert_fusion), channel_id=1, source_target_pairs={{0,8},{4,12},{8,0},{12,4},{1,9},{5,13},{9,1},{13,5},{2,10},{6,14},... | collective-permute-start | bytes 344072 | tf_op jit(solution)/shard_map/ppermute | solution.py:111
  22.4 5.1 %collective-permute-start.6 = (bf16[16,2048]{1,0:T(8,128)(2,1)S(1)}, bf16[16,2048]{1,0:T(8,128)(2,1)S(1)}, u32[]{:S(2)}, u32[]{:S(2)}) collective-permute-start(bf16[16,2048]{1,0:T(8,128)(2,1)S(1)} %add_convert_fusion.1), channel_id=1, source_target_pairs={{0,12},{4,8},{8,4},{12,0},{1,13},{5,9},{9,5},{13,1},{2,14},{6,10},... | collective-permute-start | bytes 196616 | tf_op jit(solution)/shard_map/ppermute | solution.py:111
  22.9 6.4 %collective-permute-start.1 = (bf16[1,2,128,128]{3,2,1,0:T(8,128)(2,1)S(1)}, bf16[1,2,128,128]{3,2,1,0:T(8,128)(2,1)S(1)}, u32[]{:S(2)}, u32[]{:S(2)}) collective-permute-start(bf16[1,2,128,128]{3,2,1,0:T(8,128)(2,1)S(1)} %dynamic-slice_convert_fusion), channel_id=1, source_target_pairs={{0,8},{4,12},{8,0},{12,4},{1,9},{5,13},{9,1},{13,5},{2,10},{6,14},... | collective-permute-start | bytes 196616 | tf_op jit(solution)/shard_map/ppermute | solution.py:111
  26.9 3.1 %collective-permute-start.9 = (f32[8,7168]{1,0:T(8,128)S(1)}, f32[8,7168]{1,0:T(8,128)S(1)}, u32[]{:S(2)}, u32[]{:S(2)}) collective-permute-start(f32[8,7168]{1,0:T(8,128)S(1)} %convert_add_fusion), channel_id=1, source_target_pairs={{0,4},{4,0},{8,12},{12,8},{1,5},{5,1},{9,13},{13,9},{2,6},{6,2},{1... | collective-permute-start | bytes 688136 | tf_op jit(solution)/shard_map/ppermute | solution.py:111

commit v3 on v2

v3 whole, which is shorter than its diff:
```python
import functools
import itertools

import jax
import jax.numpy as jnp
from jax import lax
from jax.experimental import pallas as pl
from jax.experimental.pallas import tpu as pltpu
from jax.sharding import PartitionSpec as P

BLK = 128
COT_CHUNK = 1024
AHEAD = 5
RADIX = 4
CROSS = 1
DOWN_WEIGHT = 40
ACT_CHUNK = 1024
LAST_LAST = (((1,), (1,)), ((), ()))
LAST_FIRST = (((1,), (0,)), ((), ()))
FIRST_FIRST = (((0,), (0,)), ((), ()))
IN_HBM = pl.BlockSpec(memory_space=pltpu.HBM)
IN_VMEM = pl.BlockSpec(memory_space=pltpu.VMEM)


def dot(a, b, dims):
    return lax.dot_general(a, b, dims, preferred_element_type=jnp.float32)


def call(kernel, outs, specs, args, scratch=(), vmem=4, flops=0, moved=0):
    return pl.pallas_call(
        kernel,
        out_shape=outs,
        in_specs=specs,
        out_specs=jax.tree.map(lambda _: IN_VMEM, outs),
        scratch_shapes=scratch,
        cost_estimate=pl.CostEstimate(flops=flops, bytes_accessed=moved, transcendentals=0),
        compiler_params=pltpu.CompilerParams(vmem_limit_bytes=vmem * 2**20),
    )(*args)


def local_kernel(rows_hbm, cols_hbm, acts, cot, down, up, sum_mine, sum_other, back,
                  rows, cols, acts_here, cot_here, down_here, up_here, act_sems, cot_sems, sems):
    dp, core = lax.axis_size("dp"), lax.rem(lax.axis_index("dp"), 2)
    width, features = acts.shape[1], cot.shape[1]
    act_step, cot_step = min(ACT_CHUNK, width), min(COT_CHUNK, features)

    def stream(source, target, step, sem):
        chunks = [pl.ds(j * step, step) for j in range(source.shape[1] // step)]
        return [pltpu.make_async_copy(source.at[:, at], target.at[:, at], sem.at[j]) for j, at in enumerate(chunks)]

    factors = [
        pltpu.make_async_copy(down, down_here, sems.at[0]),
        pltpu.make_async_copy(up, up_here, sems.at[1]),
        pltpu.make_async_copy(rows_hbm, rows, sems.at[2]),
        pltpu.make_async_copy(cols_hbm, cols, sems.at[3]),
    ]
    act_copies = stream(acts, acts_here, act_step, act_sems)
    cot_copies = stream(cot, cot_here, cot_step, cot_sems)
    order = factors + act_copies + cot_copies
    for copy in order[: AHEAD + len(factors)]:
        copy.start()
    waiting = iter(order[AHEAD + len(factors) :])

    def arrive(copy):
        copy.wait()
        for later in itertools.islice(waiting, 1):
            later.start()

    for copy in factors:
        copy.wait()
    low = None
    for j, copy in enumerate(act_copies):
        arrive(copy)
        at = pl.ds(j * act_step, act_step)
        part = dot(down_here[:, at], acts_here[:, at], LAST_LAST)
        low = part if low is None else low + part
    low = low.astype(jnp.bfloat16)
    total = None
    for j, copy in enumerate(cot_copies):
        arrive(copy)
        at = pl.ds(j * cot_step, cot_step)
        part = dot(up_here[:, at], cot_here[:, at], LAST_LAST)
        total = part if total is None else total + part
        part = dot(low, cot_here[:, at], LAST_FIRST)
        first, second = part[: part.shape[0] // 2], part[part.shape[0] // 2 :]
        sum_mine[:, at] = jnp.where(core == 0, first, second)
        sum_other[:, at] = jnp.where(core == 0, second, first)
    back[...] = total
    chips, own = dp // 2, rows.shape[1] // dp
    for out, owner in ((sum_other, 1 - core), (sum_mine, core)):
        for chip in range(chips):
            for k in range(own):
                s = (2 * chip + owner) * own + k
                r = pl.ds(pl.multiple_of(rows[0, s] * BLK, BLK), BLK)
                c = pl.ds(pl.multiple_of(cols[0, s] * BLK, BLK), BLK)
                product = dot(acts_here[:, r], cot_here[:, c], FIRST_FIRST)
                for t in range(BLK // 8):
                    at = features + ((chip * own + k) * (BLK // 8) + t) * BLK
                    out[:, at : at + BLK] = product[8 * t : 8 * t + 8]


def fetch_kernel(acts, _, out, sems):
    width, parts = out.shape[1], sems.shape[0]
    at = pl.ds(pl.multiple_of(lax.axis_index("panel") * width, width), width)
    rows = out.shape[0] // parts
    copies = []
    for j in range(parts):
        part = pl.ds(j * rows, rows)
        copies.append(pltpu.make_async_copy(acts.at[part, at], out.at[part, :], sems.at[j]))
        copies[-1].start()
    for copy in copies:
        copy.wait()


def down_kernel(*refs):
    *shares, acts, out = refs
    back = shares[0][...]
    for share in shares[1:]:
        back = back + share[...]
    out[...] = dot(back.astype(jnp.bfloat16), acts[...], LAST_FIRST)


def add_kernel(a, b, out):
    out[...] = a[...] + b[...]


def swap(x, axis, bits):
    return lax.ppermute(x, axis, [(i, i ^ bits) for i in range(lax.axis_size(axis))])


def body(acts, cot, down, up, rows, cols, live):
    tokens, width = acts.shape
    features = cot.shape[1]
    slots = rows.shape[1]
    rank = down.shape[0]
    dp, panels = lax.axis_size("dp"), lax.axis_size("panel")
    me = lax.axis_index("dp")
    core, own, mine = me % 2, slots // dp, width // panels
    f32, bf16 = jnp.float32, jnp.bfloat16
    far = [1 << b for b in range(1, dp.bit_length() - 1)]
    wire = bf16 if len(far) == 1 else f32

    hbm = functools.partial(pltpu.with_memory_space_constraint, memory_space=pltpu.HBM)
    vmem = functools.partial(pltpu.with_memory_space_constraint, memory_space=pltpu.VMEM)
    half, blk = rank // 2, BLK * BLK // 8
    here, there, back = call(
        local_kernel,
        (
            pltpu.VMEM((half, features + slots // 2 * blk), f32),
            pltpu.VMEM((half, features + slots // 2 * blk), f32),
            pltpu.VMEM((rank, tokens), f32),
        ),
        [IN_HBM] * 6,
        (hbm(rows), hbm(cols), hbm(acts), hbm(cot), hbm(down), hbm(up)),
        [
            pltpu.SMEM((1, slots), jnp.int32),
            pltpu.SMEM((1, slots), jnp.int32),
            pltpu.VMEM((tokens, width), bf16),
            pltpu.VMEM((tokens, features), bf16),
            pltpu.VMEM((rank, width), bf16),
            pltpu.VMEM((rank, features), bf16),
            pltpu.SemaphoreType.DMA((width // min(ACT_CHUNK, width),)),
            pltpu.SemaphoreType.DMA((features // min(COT_CHUNK, features),)),
            pltpu.SemaphoreType.DMA((4,)),
        ],
        vmem=24,
        flops=2 * 256 * tokens * (2 * features + width),
        moved=2 * tokens * (features + width),
    )

    bit, shares = 1, [back]
    while bit < panels:
        base = functools.reduce(jnp.add, shares)
        radix = min(RADIX, panels // bit)
        shares = [base] + [swap(base, "panel", k * bit) for k in reversed(range(1, radix))]
        bit *= radix
    got = swap(there, "dp", 1)
    total = call(
        add_kernel, pltpu.VMEM(here.shape, f32), [IN_VMEM] * 2, (vmem(here), vmem(got)), moved=3 * 4 * here.size
    )
    gu, blocks = total[:, :features], total[:, features:]
    first = None
    for b in reversed(far):
        width_left = blocks.shape[1] // 2
        side = (me // b) % 2
        away = lax.dynamic_slice_in_dim(blocks, (1 - side) * width_left, width_left, 1)
        stay = lax.dynamic_slice_in_dim(blocks, side * width_left, width_left, 1)
        sent = jnp.concatenate([gu.astype(wire), away.astype(wire)], 1)
        first = sent if first is None else first
        got = swap(sent, "dp", b)
        last, got = got, got.astype(f32)
        gu, blocks = sent[:, :features].astype(f32) + got[:, :features], stay + got[:, features:]
    blocks = blocks.reshape(8, own, BLK // 8, BLK).transpose(1, 2, 0, 3).reshape(own, BLK, BLK)
    alive = me * own + jnp.arange(own, dtype=jnp.int32) < live[0]
    blocks = jnp.where(alive[:, None, None], blocks, f32(0.0))
    other = swap(gu, "dp", 1)
    grad_up = jnp.where(core == 0, jnp.concatenate([gu, other]), jnp.concatenate([other, gu]))

    acts_mine = call(
        fetch_kernel,
        pltpu.VMEM((tokens, mine), bf16),
        [IN_HBM, pl.BlockSpec(memory_space=pl.ANY)],
        (hbm(acts), first),
        [pltpu.SemaphoreType.DMA((4,))],
        moved=2 * 2 * tokens * mine,
    )
    gd = call(
        down_kernel,
        pltpu.VMEM((rank, mine), f32),
        [IN_VMEM] * (len(shares) + 1),
        (*shares, vmem(acts_mine)),
        flops=DOWN_WEIGHT * 2 * 256 * tokens * mine,
        moved=2 * tokens * mine,
    )
    gd = gd + swap(gd, "dp", 1)
    gd, last = lax.optimization_barrier((gd, last))
    for b in far:
        sent = gd.astype(wire)
        got = swap(sent, "dp", b ^ CROSS)
        if b == far[-1]:
            got, blocks, grad_up = lax.optimization_barrier((got, blocks, grad_up))
        gd = sent.astype(f32) + got.astype(f32)
    return blocks[None], gd, grad_up


def solution(mesh):
    in_specs = (
        P(("job", "dp"), None),
        P(("job", "dp"), "panel"),
        P("job", None),
        P("job", "panel"),
        P(("job", "panel"), None),
        P(("job", "panel"), None),
        P(("job", "panel")),
    )
    out_specs = (P(("job", "panel"), "dp", None, None), P("job", "panel"), P("job", "panel"))
    return jax.shard_map(body, mesh=mesh, in_specs=in_specs, out_specs=out_specs, check_vma=False)
```

time: 31 us -> 26.4 us (0.85)
  waiting for transfers between devices: 7.5 us -> 2.61 us
  Pallas kernels: 9.21 us -> 10.6 us
  other arithmetic: 3.26 us -> 2.32 us
    ppermute x10 -> x8, waiting for transfers between devices: 7.5 us -> 2.61 us  [swap(): lax.ppermute(x, axis, [(i, i ^ bits) for i in range(lax.axis_size(axis))])]
    pallas_call x2 -> x4, Pallas kernels: 9.21 us -> 10.6 us  [call(): pl.pallas_call(kernel, out_shape=outs, in_specs=specs, out_specs=jax.tree...]
    convert_element_type x2 -> x1, other arithmetic: 1 us -> 0.03 us  [body(): last, got = (got, got.astype(f32))]
    ppermute x10 -> x8, starting transfers between devices: 9.45 us -> 9.27 us  [swap(): lax.ppermute(x, axis, [(i, i ^ bits) for i in range(lax.axis_size(axis))])]
    add x3 -> x4, other arithmetic: 0.73 us -> 0.74 us  [the longest x1 0.67 us: body(): gd = sent.astype(f32) + got.astype(f32)]
  transfers between devices with their start and end apart: 10 -> 8, of which waited for: 5 -> 4; matrix products, arithmetic and copies ran while one was open for 8% -> 6% of each run, Pallas kernels for 1% -> 8%
where the time goes in v3:
time: 26.4 us; the launch traced here: 26.2 us
  Pallas kernels  10.6 us (40%)
  starting transfers between devices  9.27 us (35%)
  waiting for transfers between devices  2.61 us (10%)
  other arithmetic  2.32 us (9%)
  between operations  1.4 us (5%)
    pallas_call x4, Pallas kernels, call(): pl.pallas_call(kernel, out_shape=outs, in_specs=specs, out_specs=jax.tree...  10.6 us
    ppermute x8, starting transfers between devices, swap(): lax.ppermute(x, axis, [(i, i ^ bits) for i in range(lax.axis_size(axis))])  9.27 us
    ppermute x8, waiting for transfers between devices, swap(): lax.ppermute(x, axis, [(i, i ^ bits) for i in range(lax.axis_size(axis))])  2.61 us
    select_n x1, other arithmetic, body(): jnp.where(core == 0, jnp.concatenate([gu, other]), jnp.concatenate([other...  0.8 us
    select_n x1, other arithmetic, body(): blocks = jnp.where(alive[:, None, None], blocks, f32(0.0))  0.73 us
    add x1, other arithmetic, body(): gd = sent.astype(f32) + got.astype(f32)  0.67 us
  transfers between devices with their start and end apart: 8, of which 4 were waited for; matrix products, arithmetic and copies ran while one was open for 6% of the time, Pallas kernels for 8%

profile of v3, /device:TPU:0, one launch (start us, length us, event | category | flops | bytes accessed | tf_op | source)
XLA Modules:
  0.0 26.2 jit_solution(7249109318798706516)
XLA Ops:
  0.6 8.6 %shard_map.94 = (f32[8,15360]{1,0:T(8,128)S(1)}, f32[8,15360]{1,0:T(8,128)S(1)}, f32[16,512]{1,0:T(8,128)S(1)}) custom-call(s32[1,8]{1,0:T(1,128)} %rows_hbm.1, s32[1,8]{1,0:T(1,128)} %cols_hbm.1, bf16[512,8192]{1,0:T(8,128)(2,1)} %acts.3, bf16[512,7168]{1,0:T(8,128)(2,1)} %cot.1, bf16[16,8192]{1,0:T(8,128)(2,1)} %down.1, bf16[16,7168]{1,0:T(8,128)(2,1)} %up.1), custom_call_target="tpu_custom_call" | custom-call | flops 5905580032 | bytes 15728640 | tf_op jit(solution)/shard_map/pallas_call | solution.py:30
  9.2 0.5 %collective-permute-start.3 = (f32[8,15360]{1,0:T(8,128)S(1)}, f32[8,15360]{1,0:T(8,128)S(1)}, u32[]{:S(2)}, u32[]{:S(2)}) collective-permute-start(f32[8,15360]{1,0:T(8,128)S(1)} %get-tuple-element.12), channel_id=1, source_target_pairs={{0,4},{4,0},{8,12},{12,8},{1,5},{5,1},{9,13},{13,9},{2,6},{6,2},{1... | collective-permute-start | bytes 1474568 | tf_op jit(solution)/shard_map/ppermute | solution.py:128
  9.7 4.7 %collective-permute-start = (f32[16,512]{1,0:T(8,128)S(1)}, f32[16,512]{1,0:T(8,128)S(1)}, u32[]{:S(2)}, u32[]{:S(2)}) collective-permute-start(f32[16,512]{1,0:T(8,128)S(1)} %get-tuple-element.10.refs_0_), channel_id=1, source_target_pairs={{0,3},{1,2},{2,1},{3,0},{4,7},{5,6},{6,5},{7,4},{8,11},{9,10},{10,... | collective-permute-start | bytes 98312 | tf_op jit(solution)/shard_map/ppermute | solution.py:128
  14.4 0.0 collective-permute-start.1
  14.4 0.6 %collective-permute-start.2 = (f32[16,512]{1,0:T(8,128)S(1)}, f32[16,512]{1,0:T(8,128)S(1)}, u32[]{:S(2)}, u32[]{:S(2)}) collective-permute-start(f32[16,512]{1,0:T(8,128)S(1)} %get-tuple-element.10.refs_0_), channel_id=1, source_target_pairs={{0,1},{1,0},{2,3},{3,2},{4,5},{5,4},{6,7},{7,6},{8,9},{9,8},{10,11... | collective-permute-start | bytes 98312 | tf_op jit(solution)/shard_map/ppermute | solution.py:128
  15.1 0.0 collective-permute-done.3.b
  15.1 0.1 shard_map.95
  15.2 1.7 %collective-permute-start.5 = (bf16[8,11264]{1,0:T(8,128)(2,1)S(1)}, bf16[8,11264]{1,0:T(8,128)(2,1)S(1)}, u32[]{:S(2)}, u32[]{:S(2)}) collective-permute-start(bf16[8,11264]{1,0:T(8,128)(2,1)S(1)} %pad_maximum_fusion._), channel_id=1, source_target_pairs={{0,8},{4,12},{8,0},{12,4},{1,9},{5,13},{9,1},{13,5},{2,10},{6,14},... | collective-permute-start | bytes 540680 | tf_op jit(solution)/shard_map/ppermute | solution.py:128
  16.9 1.6 %shard_map.96.refs_4_ = bf16[512,2048]{1,0:T(8,128)(2,1)S(1)} custom-call(bf16[512,8192]{1,0:T(8,128)(2,1)} %acts.3, bf16[8,11264]{1,0:T(8,128)(2,1)S(1)} %pad_maximum_fusion._), custom_call_target="tpu_custom_call" | custom-call | bytes 4194304 | tf_op jit(solution)/shard_map/pallas_call | solution.py:30
  18.5 0.0 collective-permute-done.refs_1_
  18.5 0.7 %collective-permute-done.1.refs_2_ = f32[16,512]{1,0:T(8,128)S(1)} collective-permute-done((f32[16,512]{1,0:T(8,128)S(1)}, f32[16,512]{1,0:T(8,128)S(1)}, u32[]{:S(2)}, u32[]{:S(2)}) %collective-permute-start.1) | collective-permute-done | bytes 32800 | tf_op jit(solution)/shard_map/ppermute | solution.py:128
  19.2 0.0 collective-permute-done.2.refs_3_
  19.2 0.4 %shard_map.97 = f32[16,2048]{1,0:T(8,128)S(1)} custom-call(f32[16,512]{1,0:T(8,128)S(1)} %get-tuple-element.10.refs_0_, f32[16,512]{1,0:T(8,128)S(1)} %collective-permute-done.refs_1_, f32[16,512]{1,0:T(8,128)S(1)} %collective-permute-done.1.refs_2_, f32[16,512]{1,0:T(8,128)S(1)} %collective-permute-done.2.refs_3_, bf16[512,2048]{1,0:T(8,128)(2,1)S(1)} %shard_map.96.refs_4_), custom_call_target="tpu_custom_call" | custom-call | flops 21474836480 | bytes 2097152 | tf_op jit(solution)/shard_map/pallas_call | solution.py:30
  19.6 0.0 collective-permute-start.4
  20.3 0.7 %collective-permute-done.4 = f32[16,2048]{1,0:T(8,128)S(1)} collective-permute-done((f32[16,2048]{1,0:T(8,128)S(1)}, f32[16,2048]{1,0:T(8,128)S(1)}, u32[]{:S(2)}, u32[]{:S(2)}) %collective-permute-start.4) | collective-permute-done | bytes 131104 | tf_op jit(solution)/shard_map/ppermute | solution.py:128
  21.0 0.5 %collective-permute-done.5 = bf16[8,11264]{1,0:T(8,128)(2,1)S(1)} collective-permute-done((bf16[8,11264]{1,0:T(8,128)(2,1)S(1)}, bf16[8,11264]{1,0:T(8,128)(2,1)S(1)}, u32[]{:S(2)}, u32[]{:S(2)}) %collective-permute-start.5) | collective-permute-done | bytes 180256 | tf_op jit(solution)/shard_map/ppermute | solution.py:128
  21.6 0.1 collective-permute-start.7
  21.7 1.7 %collective-permute-start.6 = (bf16[16,2048]{1,0:T(8,128)(2,1)S(1)}, bf16[16,2048]{1,0:T(8,128)(2,1)S(1)}, u32[]{:S(2)}, u32[]{:S(2)}) collective-permute-start(bf16[16,2048]{1,0:T(8,128)(2,1)S(1)} %add.38), channel_id=1, source_target_pairs={{0,12},{4,8},{8,4},{12,0},{1,13},{5,9},{9,5},{13,1},{2,14},{6,10},... | collective-permute-start | bytes 196616 | tf_op jit(solution)/shard_map/ppermute | solution.py:128
  23.4 0.7 %broadcast_select_fusion = f32[2,128,128]{2,1,0:T(8,128)} fusion(f32[2,128,128]{2,1,0:T(8,128)S(1)} %bitcast.8, pred[2]{0:T(512)(128)(4,1)S(1)} %add_compare_fusion), kind=kLoop, calls=%fused_computation.7 | loop fusion | flops 32768 | bytes 262146 | tf_op jit(solution)/shard_map/jit(_where)/select_n | solution.py:195
  24.1 0.0 collective-permute-done.7
  24.1 0.8 %maximum_select_fusion = f32[16,7168]{1,0:T(8,128)} fusion(f32[8,7168]{1,0:T(8,128)S(1)} %collective-permute-done.7, f32[8,7168]{1,0:T(8,128)S(1)} %slice_add_fusion, pred[]{:T(512)S(6)} %eq.6), kind=kLoop, calls=%fused_computation | loop fusion | flops 344064 | bytes 917505 | tf_op jit(solution)/shard_map/jit(_where)/select_n | solution.py:197
  24.9 0.6 %collective-permute-done.6 = bf16[16,2048]{1,0:T(8,128)(2,1)S(1)} collective-permute-done((bf16[16,2048]{1,0:T(8,128)(2,1)S(1)}, bf16[16,2048]{1,0:T(8,128)(2,1)S(1)}, u32[]{:S(2)}, u32[]{:S(2)}) %collective-permute-start.6) | collective-permute-done | bytes 65568 | tf_op jit(solution)/shard_map/ppermute | solution.py:128
  25.5 0.7 %convert_add_fusion = f32[16,2048]{1,0:T(8,128)} fusion(bf16[16,2048]{1,0:T(8,128)(2,1)S(1)} %collective-permute-done.6, bf16[16,2048]{1,0:T(8,128)(2,1)S(1)} %add.38), kind=kLoop, calls=%fused_computation.5 | loop fusion | flops 98304 | bytes 262144 | tf_op jit(solution)/shard_map/add | solution.py:222
  (9 shorter events, 0.2 us)
Async XLA Ops:
  9.2 5.8 %collective-permute-start.3 = (f32[8,15360]{1,0:T(8,128)S(1)}, f32[8,15360]{1,0:T(8,128)S(1)}, u32[]{:S(2)}, u32[]{:S(2)}) collective-permute-start(f32[8,15360]{1,0:T(8,128)S(1)} %get-tuple-element.12), channel_id=1, source_target_pairs={{0,4},{4,0},{8,12},{12,8},{1,5},{5,1},{9,13},{13,9},{2,6},{6,2},{1... | collective-permute-start | bytes 1474568 | tf_op jit(solution)/shard_map/ppermute | solution.py:128
  9.7 8.7 %collective-permute-start = (f32[16,512]{1,0:T(8,128)S(1)}, f32[16,512]{1,0:T(8,128)S(1)}, u32[]{:S(2)}, u32[]{:S(2)}) collective-permute-start(f32[16,512]{1,0:T(8,128)S(1)} %get-tuple-element.10.refs_0_), channel_id=1, source_target_pairs={{0,3},{1,2},{2,1},{3,0},{4,7},{5,6},{6,5},{7,4},{8,11},{9,10},{10,... | collective-permute-start | bytes 98312 | tf_op jit(solution)/shard_map/ppermute | solution.py:128
  14.4 4.8 %collective-permute-start.1 = (f32[16,512]{1,0:T(8,128)S(1)}, f32[16,512]{1,0:T(8,128)S(1)}, u32[]{:S(2)}, u32[]{:S(2)}) collective-permute-start(f32[16,512]{1,0:T(8,128)S(1)} %get-tuple-element.10.refs_0_), channel_id=1, source_target_pairs={{0,2},{1,3},{2,0},{3,1},{4,6},{5,7},{6,4},{7,5},{8,10},{9,11},{10,... | collective-permute-start | bytes 98312 | tf_op jit(solution)/shard_map/ppermute | solution.py:128
  14.4 4.8 %collective-permute-start.2 = (f32[16,512]{1,0:T(8,128)S(1)}, f32[16,512]{1,0:T(8,128)S(1)}, u32[]{:S(2)}, u32[]{:S(2)}) collective-permute-start(f32[16,512]{1,0:T(8,128)S(1)} %get-tuple-element.10.refs_0_), channel_id=1, source_target_pairs={{0,1},{1,0},{2,3},{3,2},{4,5},{5,4},{6,7},{7,6},{8,9},{9,8},{10,11... | collective-permute-start | bytes 98312 | tf_op jit(solution)/shard_map/ppermute | solution.py:128
  15.2 6.3 %collective-permute-start.5 = (bf16[8,11264]{1,0:T(8,128)(2,1)S(1)}, bf16[8,11264]{1,0:T(8,128)(2,1)S(1)}, u32[]{:S(2)}, u32[]{:S(2)}) collective-permute-start(bf16[8,11264]{1,0:T(8,128)(2,1)S(1)} %pad_maximum_fusion._), channel_id=1, source_target_pairs={{0,8},{4,12},{8,0},{12,4},{1,9},{5,13},{9,1},{13,5},{2,10},{6,14},... | collective-permute-start | bytes 540680 | tf_op jit(solution)/shard_map/ppermute | solution.py:128
  19.6 1.4 %collective-permute-start.4 = (f32[16,2048]{1,0:T(8,128)S(1)}, f32[16,2048]{1,0:T(8,128)S(1)}, u32[]{:S(2)}, u32[]{:S(2)}) collective-permute-start(f32[16,2048]{1,0:T(8,128)S(1)} %shard_map.97), channel_id=1, source_target_pairs={{0,4},{4,0},{8,12},{12,8},{1,5},{5,1},{9,13},{13,9},{2,6},{6,2},{1... | collective-permute-start | bytes 393224 | tf_op jit(solution)/shard_map/ppermute | solution.py:128
  21.6 2.5 %collective-permute-start.7 = (f32[8,7168]{1,0:T(8,128)S(1)}, f32[8,7168]{1,0:T(8,128)S(1)}, u32[]{:S(2)}, u32[]{:S(2)}) collective-permute-start(f32[8,7168]{1,0:T(8,128)S(1)} %slice_add_fusion), channel_id=1, source_target_pairs={{0,4},{4,0},{8,12},{12,8},{1,5},{5,1},{9,13},{13,9},{2,6},{6,2},{1... | collective-permute-start | bytes 688136 | tf_op jit(solution)/shard_map/ppermute | solution.py:128
  21.7 3.8 %collective-permute-start.6 = (bf16[16,2048]{1,0:T(8,128)(2,1)S(1)}, bf16[16,2048]{1,0:T(8,128)(2,1)S(1)}, u32[]{:S(2)}, u32[]{:S(2)}) collective-permute-start(bf16[16,2048]{1,0:T(8,128)(2,1)S(1)} %add.38), channel_id=1, source_target_pairs={{0,12},{4,8},{8,4},{12,0},{1,13},{5,9},{9,5},{13,1},{2,14},{6,10},... | collective-permute-start | bytes 196616 | tf_op jit(solution)/shard_map/ppermute | solution.py:128

commit v4 on v3

--- a/solution.py
+++ b/solution.py
@@ -10,10 +10,11 @@
 
 BLK = 128
 COT_CHUNK = 1024
-AHEAD = 5
-RADIX = 4
+AHEAD = 4
+GROW = 2
+RADIX = 2
 CROSS = 1
-DOWN_WEIGHT = 40
+DOWN_WEIGHT = 0
 ACT_CHUNK = 1024
 LAST_LAST = (((1,), (1,)), ((), ()))
 LAST_FIRST = (((1,), (0,)), ((), ()))
@@ -63,7 +64,7 @@
 
     def arrive(copy):
         copy.wait()
-        for later in itertools.islice(waiting, 1):
+        for later in itertools.islice(waiting, GROW):
             later.start()
 
     for copy in factors:
@@ -74,7 +75,8 @@
         at = pl.ds(j * act_step, act_step)
         part = dot(down_here[:, at], acts_here[:, at], LAST_LAST)
         low = part if low is None else low + part
-    low = low.astype(jnp.bfloat16)
+    rank = low.shape[0]
+    low = jnp.where(core == 0, low, jnp.concatenate([low[rank // 2 :], low[: rank // 2]])).astype(jnp.bfloat16)
     total = None
     for j, copy in enumerate(cot_copies):
         arrive(copy)
@@ -82,9 +84,8 @@
         part = dot(up_here[:, at], cot_here[:, at], LAST_LAST)
         total = part if total is None else total + part
         part = dot(low, cot_here[:, at], LAST_FIRST)
-        first, second = part[: part.shape[0] // 2], part[part.shape[0] // 2 :]
-        sum_mine[:, at] = jnp.where(core == 0, first, second)
-        sum_other[:, at] = jnp.where(core == 0, second, first)
+        sum_mine[:, at] = part[: rank // 2]
+        sum_other[:, at] = part[rank // 2 :]
     back[...] = total
     chips, own = dp // 2, rows.shape[1] // dp
     for out, owner in ((sum_other, 1 - core), (sum_mine, core)):
@@ -168,12 +169,6 @@
         moved=2 * tokens * (features + width),
     )
 
-    bit, shares = 1, [back]
-    while bit < panels:
-        base = functools.reduce(jnp.add, shares)
-        radix = min(RADIX, panels // bit)
-        shares = [base] + [swap(base, "panel", k * bit) for k in reversed(range(1, radix))]
-        bit *= radix
     got = swap(there, "dp", 1)
     total = call(
         add_kernel, pltpu.VMEM(here.shape, f32), [IN_VMEM] * 2, (vmem(here), vmem(got)), moved=3 * 4 * here.size
@@ -196,11 +191,19 @@
     other = swap(gu, "dp", 1)
     grad_up = jnp.where(core == 0, jnp.concatenate([gu, other]), jnp.concatenate([other, gu]))
 
+    bit, shares = 1, [back]
+    while bit < panels:
+        if bit > 1:
+            shares[-1], first = lax.optimization_barrier((shares[-1], first))
+        base = functools.reduce(jnp.add, shares)
+        radix = min(RADIX, panels // bit)
+        shares = [base] + [swap(base, "panel", (panels // 2) // bit) for k in reversed(range(1, radix))]
+        bit *= radix
     acts_mine = call(
         fetch_kernel,
         pltpu.VMEM((tokens, mine), bf16),
         [IN_HBM, pl.BlockSpec(memory_space=pl.ANY)],
-        (hbm(acts), first),
+        (hbm(acts), shares[0]),
         [pltpu.SemaphoreType.DMA((4,))],
         moved=2 * 2 * tokens * mine,
     )

time: 26.4 us -> 26.2 us (level)
  waiting for transfers between devices: 2.61 us -> 2.21 us
    ppermute x8 -> x7, waiting for transfers between devices: 2.61 us -> 2.21 us  [swap(): lax.ppermute(x, axis, [(i, i ^ bits) for i in range(lax.axis_size(axis))])]
    ppermute x8 -> x7, starting transfers between devices: 9.27 us -> 9.46 us  [swap(): lax.ppermute(x, axis, [(i, i ^ bits) for i in range(lax.axis_size(axis))])]
  transfers between devices with their start and end apart: 8 -> 7, of which waited for: 4 -> 4; matrix products, arithmetic and copies ran while one was open for 6% -> 6% of each run, Pallas kernels for 8% -> 8%
where the time goes in v4:
time: 26.2 us; the launch traced here: 26 us
  Pallas kernels  10.6 us (40%)
  starting transfers between devices  9.46 us (36%)
  other arithmetic  2.33 us (9%)
  waiting for transfers between devices  2.21 us (8%)
  between operations  1.39 us (5%)
    pallas_call x4, Pallas kernels, call(): pl.pallas_call(kernel, out_shape=outs, in_specs=specs, out_specs=jax.tree...  10.6 us
    ppermute x7, starting transfers between devices, swap(): lax.ppermute(x, axis, [(i, i ^ bits) for i in range(lax.axis_size(axis))])  9.46 us
    ppermute x7, waiting for transfers between devices, swap(): lax.ppermute(x, axis, [(i, i ^ bits) for i in range(lax.axis_size(axis))])  2.21 us
    select_n x1, other arithmetic, body(): jnp.where(core == 0, jnp.concatenate([gu, other]), jnp.concatenate([other...  0.8 us
    select_n x1, other arithmetic, body(): blocks = jnp.where(alive[:, None, None], blocks, f32(0.0))  0.73 us
    add x1, other arithmetic, body(): gd = sent.astype(f32) + got.astype(f32)  0.67 us
  transfers between devices with their start and end apart: 7, of which 4 were waited for; matrix products, arithmetic and copies ran while one was open for 6% of the time, Pallas kernels for 8%

profile of v4, /device:TPU:0, one launch (start us, length us, event | category | flops | bytes accessed | tf_op | source)
XLA Modules:
  0.0 26.0 jit_solution(7944540843143059604)
XLA Ops:
  0.6 8.6 %shard_map.94 = (f32[8,15360]{1,0:T(8,128)S(1)}, f32[8,15360]{1,0:T(8,128)S(1)}, f32[16,512]{1,0:T(8,128)S(1)}) custom-call(s32[1,8]{1,0:T(1,128)} %rows_hbm.1, s32[1,8]{1,0:T(1,128)} %cols_hbm.1, bf16[512,8192]{1,0:T(8,128)(2,1)} %acts.3, bf16[512,7168]{1,0:T(8,128)(2,1)} %cot.1, bf16[16,8192]{1,0:T(8,128)(2,1)} %down.1, bf16[16,7168]{1,0:T(8,128)(2,1)} %up.1), custom_call_target="tpu_custom_call" | custom-call | flops 5905580032 | bytes 15728640 | tf_op jit(solution)/shard_map/pallas_call | solution.py:31
  9.2 0.5 %collective-permute-start.1 = (f32[8,15360]{1,0:T(8,128)S(1)}, f32[8,15360]{1,0:T(8,128)S(1)}, u32[]{:S(2)}, u32[]{:S(2)}) collective-permute-start(f32[8,15360]{1,0:T(8,128)S(1)} %get-tuple-element.13), channel_id=1, source_target_pairs={{0,4},{4,0},{8,12},{12,8},{1,5},{5,1},{9,13},{13,9},{2,6},{6,2},{1... | collective-permute-start | bytes 1474568 | tf_op jit(solution)/shard_map/ppermute | solution.py:129
  9.7 3.7 %collective-permute-start = (f32[16,512]{1,0:T(8,128)S(1)}, f32[16,512]{1,0:T(8,128)S(1)}, u32[]{:S(2)}, u32[]{:S(2)}) collective-permute-start(f32[16,512]{1,0:T(8,128)S(1)} %get-tuple-element.11), channel_id=1, source_target_pairs={{0,2},{1,3},{2,0},{3,1},{4,6},{5,7},{6,4},{7,5},{8,10},{9,11},{10,... | collective-permute-start | bytes 98312 | tf_op jit(solution)/shard_map/ppermute | solution.py:129
  13.4 0.0 collective-permute-done.1.b
  13.4 0.1 shard_map.95
  13.6 1.6 %collective-permute-start.4 = (bf16[8,11264]{1,0:T(8,128)(2,1)S(1)}, bf16[8,11264]{1,0:T(8,128)(2,1)S(1)}, u32[]{:S(2)}, u32[]{:S(2)}) collective-permute-start(bf16[8,11264]{1,0:T(8,128)(2,1)S(1)} %pad_maximum_fusion), channel_id=1, source_target_pairs={{0,8},{4,12},{8,0},{12,4},{1,9},{5,13},{9,1},{13,5},{2,10},{6,14},... | collective-permute-start | bytes 540680 | tf_op jit(solution)/shard_map/ppermute | solution.py:129
  15.1 0.3 %collective-permute-done = f32[16,512]{1,0:T(8,128)S(1)} collective-permute-done((f32[16,512]{1,0:T(8,128)S(1)}, f32[16,512]{1,0:T(8,128)S(1)}, u32[]{:S(2)}, u32[]{:S(2)}) %collective-permute-start) | collective-permute-done | bytes 32800 | tf_op jit(solution)/shard_map/ppermute | solution.py:129
  15.4 1.8 %collective-permute-start.2 = (f32[16,512]{1,0:T(8,128)S(1)}, f32[16,512]{1,0:T(8,128)S(1)}, u32[]{:S(2)}, u32[]{:S(2)}) collective-permute-start(f32[16,512]{1,0:T(8,128)S(1)} %add.41._.refs_0_), channel_id=1, source_target_pairs={{0,1},{1,0},{2,3},{3,2},{4,5},{5,4},{6,7},{7,6},{8,9},{9,8},{10,11... | collective-permute-start | bytes 98312 | tf_op jit(solution)/shard_map/ppermute | solution.py:129
  17.2 1.6 %shard_map.96.refs_2_ = bf16[512,2048]{1,0:T(8,128)(2,1)S(1)} custom-call(bf16[512,8192]{1,0:T(8,128)(2,1)} %acts.3, f32[16,512]{1,0:T(8,128)S(1)} %add.41._.refs_0_), custom_call_target="tpu_custom_call" | custom-call | bytes 4194304 | tf_op jit(solution)/shard_map/pallas_call | solution.py:31
  18.8 0.5 %collective-permute-done.2.refs_1_ = f32[16,512]{1,0:T(8,128)S(1)} collective-permute-done((f32[16,512]{1,0:T(8,128)S(1)}, f32[16,512]{1,0:T(8,128)S(1)}, u32[]{:S(2)}, u32[]{:S(2)}) %collective-permute-start.2) | collective-permute-done | bytes 32800 | tf_op jit(solution)/shard_map/ppermute | solution.py:129
  19.3 0.4 %shard_map.97 = f32[16,2048]{1,0:T(8,128)S(1)} custom-call(f32[16,512]{1,0:T(8,128)S(1)} %add.41._.refs_0_, f32[16,512]{1,0:T(8,128)S(1)} %collective-permute-done.2.refs_1_, bf16[512,2048]{1,0:T(8,128)(2,1)S(1)} %shard_map.96.refs_2_), custom_call_target="tpu_custom_call" | custom-call | bytes 2097152 | tf_op jit(solution)/shard_map/pallas_call | solution.py:31
  19.7 0.0 collective-permute-start.3
  20.4 0.7 %collective-permute-done.3 = f32[16,2048]{1,0:T(8,128)S(1)} collective-permute-done((f32[16,2048]{1,0:T(8,128)S(1)}, f32[16,2048]{1,0:T(8,128)S(1)}, u32[]{:S(2)}, u32[]{:S(2)}) %collective-permute-start.3) | collective-permute-done | bytes 131104 | tf_op jit(solution)/shard_map/ppermute | solution.py:129
  21.1 0.0 collective-permute-done.4
  21.2 0.2 collective-permute-start.6
  21.4 1.7 %collective-permute-start.5 = (bf16[16,2048]{1,0:T(8,128)(2,1)S(1)}, bf16[16,2048]{1,0:T(8,128)(2,1)S(1)}, u32[]{:S(2)}, u32[]{:S(2)}) collective-permute-start(bf16[16,2048]{1,0:T(8,128)(2,1)S(1)} %add.42), channel_id=1, source_target_pairs={{0,12},{4,8},{8,4},{12,0},{1,13},{5,9},{9,5},{13,1},{2,14},{6,10},... | collective-permute-start | bytes 196616 | tf_op jit(solution)/shard_map/ppermute | solution.py:129
  23.1 0.7 %broadcast_select_fusion = f32[2,128,128]{2,1,0:T(8,128)} fusion(f32[2,128,128]{2,1,0:T(8,128)S(1)} %bitcast.8, pred[2]{0:T(512)(128)(4,1)S(1)} %add_compare_fusion), kind=kLoop, calls=%fused_computation.7 | loop fusion | flops 32768 | bytes 262146 | tf_op jit(solution)/shard_map/jit(_where)/select_n | solution.py:190
  23.8 0.0 collective-permute-done.6
  23.8 0.8 %maximum_select_fusion = f32[16,7168]{1,0:T(8,128)} fusion(f32[8,7168]{1,0:T(8,128)S(1)} %collective-permute-done.6, f32[8,7168]{1,0:T(8,128)S(1)} %slice_add_fusion, pred[]{:T(512)S(6)} %eq.6), kind=kLoop, calls=%fused_computation | loop fusion | flops 344064 | bytes 917505 | tf_op jit(solution)/shard_map/jit(_where)/select_n | solution.py:192
  24.6 0.7 %collective-permute-done.5 = bf16[16,2048]{1,0:T(8,128)(2,1)S(1)} collective-permute-done((bf16[16,2048]{1,0:T(8,128)(2,1)S(1)}, bf16[16,2048]{1,0:T(8,128)(2,1)S(1)}, u32[]{:S(2)}, u32[]{:S(2)}) %collective-permute-start.5) | collective-permute-done | bytes 65568 | tf_op jit(solution)/shard_map/ppermute | solution.py:129
  25.3 0.7 %convert_add_fusion = f32[16,2048]{1,0:T(8,128)} fusion(bf16[16,2048]{1,0:T(8,128)(2,1)S(1)} %collective-permute-done.5, bf16[16,2048]{1,0:T(8,128)(2,1)S(1)} %add.42), kind=kLoop, calls=%fused_computation.5 | loop fusion | flops 98304 | bytes 262144 | tf_op jit(solution)/shard_map/add | solution.py:225
  (10 shorter events, 0.2 us)
Async XLA Ops:
  9.2 4.2 %collective-permute-start.1 = (f32[8,15360]{1,0:T(8,128)S(1)}, f32[8,15360]{1,0:T(8,128)S(1)}, u32[]{:S(2)}, u32[]{:S(2)}) collective-permute-start(f32[8,15360]{1,0:T(8,128)S(1)} %get-tuple-element.13), channel_id=1, source_target_pairs={{0,4},{4,0},{8,12},{12,8},{1,5},{5,1},{9,13},{13,9},{2,6},{6,2},{1... | collective-permute-start | bytes 1474568 | tf_op jit(solution)/shard_map/ppermute | solution.py:129
  9.7 5.7 %collective-permute-start = (f32[16,512]{1,0:T(8,128)S(1)}, f32[16,512]{1,0:T(8,128)S(1)}, u32[]{:S(2)}, u32[]{:S(2)}) collective-permute-start(f32[16,512]{1,0:T(8,128)S(1)} %get-tuple-element.11), channel_id=1, source_target_pairs={{0,2},{1,3},{2,0},{3,1},{4,6},{5,7},{6,4},{7,5},{8,10},{9,11},{10,... | collective-permute-start | bytes 98312 | tf_op jit(solution)/shard_map/ppermute | solution.py:129
  13.6 7.5 %collective-permute-start.4 = (bf16[8,11264]{1,0:T(8,128)(2,1)S(1)}, bf16[8,11264]{1,0:T(8,128)(2,1)S(1)}, u32[]{:S(2)}, u32[]{:S(2)}) collective-permute-start(bf16[8,11264]{1,0:T(8,128)(2,1)S(1)} %pad_maximum_fusion), channel_id=1, source_target_pairs={{0,8},{4,12},{8,0},{12,4},{1,9},{5,13},{9,1},{13,5},{2,10},{6,14},... | collective-permute-start | bytes 540680 | tf_op jit(solution)/shard_map/ppermute | solution.py:129
  15.4 3.9 %collective-permute-start.2 = (f32[16,512]{1,0:T(8,128)S(1)}, f32[16,512]{1,0:T(8,128)S(1)}, u32[]{:S(2)}, u32[]{:S(2)}) collective-permute-start(f32[16,512]{1,0:T(8,128)S(1)} %add.41._.refs_0_), channel_id=1, source_target_pairs={{0,1},{1,0},{2,3},{3,2},{4,5},{5,4},{6,7},{7,6},{8,9},{9,8},{10,11... | collective-permute-start | bytes 98312 | tf_op jit(solution)/shard_map/ppermute | solution.py:129
  19.7 1.4 %collective-permute-start.3 = (f32[16,2048]{1,0:T(8,128)S(1)}, f32[16,2048]{1,0:T(8,128)S(1)}, u32[]{:S(2)}, u32[]{:S(2)}) collective-permute-start(f32[16,2048]{1,0:T(8,128)S(1)} %shard_map.97), channel_id=1, source_target_pairs={{0,4},{4,0},{8,12},{12,8},{1,5},{5,1},{9,13},{13,9},{2,6},{6,2},{1... | collective-permute-start | bytes 393224 | tf_op jit(solution)/shard_map/ppermute | solution.py:129
  21.2 2.6 %collective-permute-start.6 = (f32[8,7168]{1,0:T(8,128)S(1)}, f32[8,7168]{1,0:T(8,128)S(1)}, u32[]{:S(2)}, u32[]{:S(2)}) collective-permute-start(f32[8,7168]{1,0:T(8,128)S(1)} %slice_add_fusion), channel_id=1, source_target_pairs={{0,4},{4,0},{8,12},{12,8},{1,5},{5,1},{9,13},{13,9},{2,6},{6,2},{1... | collective-permute-start | bytes 688136 | tf_op jit(solution)/shard_map/ppermute | solution.py:129
  21.4 3.9 %collective-permute-start.5 = (bf16[16,2048]{1,0:T(8,128)(2,1)S(1)}, bf16[16,2048]{1,0:T(8,128)(2,1)S(1)}, u32[]{:S(2)}, u32[]{:S(2)}) collective-permute-start(bf16[16,2048]{1,0:T(8,128)(2,1)S(1)} %add.42), channel_id=1, source_target_pairs={{0,12},{4,8},{8,4},{12,0},{1,13},{5,9},{9,5},{13,1},{2,14},{6,10},... | collective-permute-start | bytes 196616 | tf_op jit(solution)/shard_map/ppermute | solution.py:129

commit v5 on v4

--- a/solution.py
+++ b/solution.py
@@ -188,8 +188,6 @@
     blocks = blocks.reshape(8, own, BLK // 8, BLK).transpose(1, 2, 0, 3).reshape(own, BLK, BLK)
     alive = me * own + jnp.arange(own, dtype=jnp.int32) < live[0]
     blocks = jnp.where(alive[:, None, None], blocks, f32(0.0))
-    other = swap(gu, "dp", 1)
-    grad_up = jnp.where(core == 0, jnp.concatenate([gu, other]), jnp.concatenate([other, gu]))
 
     bit, shares = 1, [back]
     while bit < panels:
@@ -217,6 +215,9 @@
     )
     gd = gd + swap(gd, "dp", 1)
     gd, last = lax.optimization_barrier((gd, last))
+    gu, _ = lax.optimization_barrier((gu, gd.astype(wire)))
+    other = swap(gu, "dp", 1)
+    grad_up = jnp.where(core == 0, jnp.concatenate([gu, other]), jnp.concatenate([other, gu]))
     for b in far:
         sent = gd.astype(wire)
         got = swap(sent, "dp", b ^ CROSS)

time: 26.2 us -> 26.1 us (level)
  transfers between devices with their start and end apart: 7 -> 7, of which waited for: 4 -> 5; matrix products, arithmetic and copies ran while one was open for 6% -> 6% of each run, Pallas kernels for 8% -> 8%
where the time goes in v5:
time: 26.1 us; the launch traced here: 26 us
  Pallas kernels  10.6 us (41%)
  starting transfers between devices  9.47 us (36%)
  other arithmetic  2.33 us (9%)
  waiting for transfers between devices  2.17 us (8%)
  between operations  1.39 us (5%)
    pallas_call x4, Pallas kernels, call(): pl.pallas_call(kernel, out_shape=outs, in_specs=specs, out_specs=jax.tree...  10.6 us
    ppermute x7, starting transfers between devices, swap(): lax.ppermute(x, axis, [(i, i ^ bits) for i in range(lax.axis_size(axis))])  9.47 us
    ppermute x7, waiting for transfers between devices, swap(): lax.ppermute(x, axis, [(i, i ^ bits) for i in range(lax.axis_size(axis))])  2.17 us
    select_n x1, other arithmetic, body(): jnp.where(core == 0, jnp.concatenate([gu, other]), jnp.concatenate([other...  0.8 us
    select_n x1, other arithmetic, body(): blocks = jnp.where(alive[:, None, None], blocks, f32(0.0))  0.73 us
    add x1, other arithmetic, body(): gd = sent.astype(f32) + got.astype(f32)  0.67 us
  transfers between devices with their start and end apart: 7, of which 5 were waited for; matrix products, arithmetic and copies ran while one was open for 6% of the time, Pallas kernels for 8%

profile of v5, /device:TPU:0, one launch (start us, length us, event | category | flops | bytes accessed | tf_op | source)
XLA Modules:
  0.0 26.0 jit_solution(18279376153094014093)
XLA Ops:
  0.6 8.6 %shard_map.94 = (f32[8,15360]{1,0:T(8,128)S(1)}, f32[8,15360]{1,0:T(8,128)S(1)}, f32[16,512]{1,0:T(8,128)S(1)}) custom-call(s32[1,8]{1,0:T(1,128)} %rows_hbm.1, s32[1,8]{1,0:T(1,128)} %cols_hbm.1, bf16[512,8192]{1,0:T(8,128)(2,1)} %acts.3, bf16[512,7168]{1,0:T(8,128)(2,1)} %cot.1, bf16[16,8192]{1,0:T(8,128)(2,1)} %down.1, bf16[16,7168]{1,0:T(8,128)(2,1)} %up.1), custom_call_target="tpu_custom_call" | custom-call | flops 5905580032 | bytes 15728640 | tf_op jit(solution)/shard_map/pallas_call | solution.py:31
  9.2 0.5 %collective-permute-start.1 = (f32[8,15360]{1,0:T(8,128)S(1)}, f32[8,15360]{1,0:T(8,128)S(1)}, u32[]{:S(2)}, u32[]{:S(2)}) collective-permute-start(f32[8,15360]{1,0:T(8,128)S(1)} %get-tuple-element.14), channel_id=1, source_target_pairs={{0,4},{4,0},{8,12},{12,8},{1,5},{5,1},{9,13},{13,9},{2,6},{6,2},{1... | collective-permute-start | bytes 1474568 | tf_op jit(solution)/shard_map/ppermute | solution.py:129
  9.7 3.7 %collective-permute-start = (f32[16,512]{1,0:T(8,128)S(1)}, f32[16,512]{1,0:T(8,128)S(1)}, u32[]{:S(2)}, u32[]{:S(2)}) collective-permute-start(f32[16,512]{1,0:T(8,128)S(1)} %get-tuple-element.12), channel_id=1, source_target_pairs={{0,2},{1,3},{2,0},{3,1},{4,6},{5,7},{6,4},{7,5},{8,10},{9,11},{10,... | collective-permute-start | bytes 98312 | tf_op jit(solution)/shard_map/ppermute | solution.py:129
  13.4 0.0 collective-permute-done.1.b
  13.4 0.1 shard_map.95
  13.6 1.6 %collective-permute-start.4 = (bf16[8,11264]{1,0:T(8,128)(2,1)S(1)}, bf16[8,11264]{1,0:T(8,128)(2,1)S(1)}, u32[]{:S(2)}, u32[]{:S(2)}) collective-permute-start(bf16[8,11264]{1,0:T(8,128)(2,1)S(1)} %pad_maximum_fusion), channel_id=1, source_target_pairs={{0,8},{4,12},{8,0},{12,4},{1,9},{5,13},{9,1},{13,5},{2,10},{6,14},... | collective-permute-start | bytes 540680 | tf_op jit(solution)/shard_map/ppermute | solution.py:129
  15.1 0.3 %collective-permute-done = f32[16,512]{1,0:T(8,128)S(1)} collective-permute-done((f32[16,512]{1,0:T(8,128)S(1)}, f32[16,512]{1,0:T(8,128)S(1)}, u32[]{:S(2)}, u32[]{:S(2)}) %collective-permute-start) | collective-permute-done | bytes 32800 | tf_op jit(solution)/shard_map/ppermute | solution.py:129
  15.4 1.8 %collective-permute-start.2 = (f32[16,512]{1,0:T(8,128)S(1)}, f32[16,512]{1,0:T(8,128)S(1)}, u32[]{:S(2)}, u32[]{:S(2)}) collective-permute-start(f32[16,512]{1,0:T(8,128)S(1)} %add.41._.refs_0_), channel_id=1, source_target_pairs={{0,1},{1,0},{2,3},{3,2},{4,5},{5,4},{6,7},{7,6},{8,9},{9,8},{10,11... | collective-permute-start | bytes 98312 | tf_op jit(solution)/shard_map/ppermute | solution.py:129
  17.2 1.6 %shard_map.96.refs_2_ = bf16[512,2048]{1,0:T(8,128)(2,1)S(1)} custom-call(bf16[512,8192]{1,0:T(8,128)(2,1)} %acts.3, f32[16,512]{1,0:T(8,128)S(1)} %add.41._.refs_0_), custom_call_target="tpu_custom_call" | custom-call | bytes 4194304 | tf_op jit(solution)/shard_map/pallas_call | solution.py:31
  18.8 0.5 %collective-permute-done.2.refs_1_ = f32[16,512]{1,0:T(8,128)S(1)} collective-permute-done((f32[16,512]{1,0:T(8,128)S(1)}, f32[16,512]{1,0:T(8,128)S(1)}, u32[]{:S(2)}, u32[]{:S(2)}) %collective-permute-start.2) | collective-permute-done | bytes 32800 | tf_op jit(solution)/shard_map/ppermute | solution.py:129
  19.3 0.4 %shard_map.97 = f32[16,2048]{1,0:T(8,128)S(1)} custom-call(f32[16,512]{1,0:T(8,128)S(1)} %add.41._.refs_0_, f32[16,512]{1,0:T(8,128)S(1)} %collective-permute-done.2.refs_1_, bf16[512,2048]{1,0:T(8,128)(2,1)S(1)} %shard_map.96.refs_2_), custom_call_target="tpu_custom_call" | custom-call | bytes 2097152 | tf_op jit(solution)/shard_map/pallas_call | solution.py:31
  19.7 0.0 collective-permute-start.3
  20.4 0.7 %collective-permute-done.3 = f32[16,2048]{1,0:T(8,128)S(1)} collective-permute-done((f32[16,2048]{1,0:T(8,128)S(1)}, f32[16,2048]{1,0:T(8,128)S(1)}, u32[]{:S(2)}, u32[]{:S(2)}) %collective-permute-start.3) | collective-permute-done | bytes 131104 | tf_op jit(solution)/shard_map/ppermute | solution.py:129
  21.1 0.0 collective-permute-done.4
  21.2 1.6 %collective-permute-start.5 = (bf16[16,2048]{1,0:T(8,128)(2,1)S(1)}, bf16[16,2048]{1,0:T(8,128)(2,1)S(1)}, u32[]{:S(2)}, u32[]{:S(2)}) collective-permute-start(bf16[16,2048]{1,0:T(8,128)(2,1)S(1)} %add.42), channel_id=1, source_target_pairs={{0,12},{4,8},{8,4},{12,0},{1,13},{5,9},{9,5},{13,1},{2,14},{6,10},... | collective-permute-start | bytes 196616 | tf_op jit(solution)/shard_map/ppermute | solution.py:129
  22.7 0.4 %collective-permute-start.6 = (f32[8,7168]{1,0:T(8,128)S(1)}, f32[8,7168]{1,0:T(8,128)S(1)}, u32[]{:S(2)}, u32[]{:S(2)}) collective-permute-start(f32[8,7168]{1,0:T(8,128)S(1)} %slice_add_fusion), channel_id=1, source_target_pairs={{0,4},{4,0},{8,12},{12,8},{1,5},{5,1},{9,13},{13,9},{2,6},{6,2},{1... | collective-permute-start | bytes 688136 | tf_op jit(solution)/shard_map/ppermute | solution.py:129
  23.1 0.7 %broadcast_select_fusion = f32[2,128,128]{2,1,0:T(8,128)} fusion(f32[2,128,128]{2,1,0:T(8,128)S(1)} %bitcast.8, pred[2]{0:T(512)(128)(4,1)S(1)} %add_compare_fusion), kind=kLoop, calls=%fused_computation.7 | loop fusion | flops 32768 | bytes 262146 | tf_op jit(solution)/shard_map/jit(_where)/select_n | solution.py:190
  23.8 0.4 %collective-permute-done.6 = f32[8,7168]{1,0:T(8,128)S(1)} collective-permute-done((f32[8,7168]{1,0:T(8,128)S(1)}, f32[8,7168]{1,0:T(8,128)S(1)}, u32[]{:S(2)}, u32[]{:S(2)}) %collective-permute-start.6) | collective-permute-done | bytes 229408 | tf_op jit(solution)/shard_map/ppermute | solution.py:129
  24.2 0.8 %maximum_select_fusion = f32[16,7168]{1,0:T(8,128)} fusion(f32[8,7168]{1,0:T(8,128)S(1)} %collective-permute-done.6, f32[8,7168]{1,0:T(8,128)S(1)} %slice_add_fusion, pred[]{:T(512)S(6)} %eq.6), kind=kLoop, calls=%fused_computation | loop fusion | flops 344064 | bytes 917505 | tf_op jit(solution)/shard_map/jit(_where)/select_n | solution.py:220
  25.0 0.3 %collective-permute-done.5 = bf16[16,2048]{1,0:T(8,128)(2,1)S(1)} collective-permute-done((bf16[16,2048]{1,0:T(8,128)(2,1)S(1)}, bf16[16,2048]{1,0:T(8,128)(2,1)S(1)}, u32[]{:S(2)}, u32[]{:S(2)}) %collective-permute-start.5) | collective-permute-done | bytes 65568 | tf_op jit(solution)/shard_map/ppermute | solution.py:129
  25.3 0.7 %convert_add_fusion = f32[16,2048]{1,0:T(8,128)} fusion(bf16[16,2048]{1,0:T(8,128)(2,1)S(1)} %collective-permute-done.5, bf16[16,2048]{1,0:T(8,128)(2,1)S(1)} %add.42), kind=kLoop, calls=%fused_computation.5 | loop fusion | flops 98304 | bytes 262144 | tf_op jit(solution)/shard_map/add | solution.py:226
  (10 shorter events, 0.2 us)
Async XLA Ops:
  9.2 4.2 %collective-permute-start.1 = (f32[8,15360]{1,0:T(8,128)S(1)}, f32[8,15360]{1,0:T(8,128)S(1)}, u32[]{:S(2)}, u32[]{:S(2)}) collective-permute-start(f32[8,15360]{1,0:T(8,128)S(1)} %get-tuple-element.14), channel_id=1, source_target_pairs={{0,4},{4,0},{8,12},{12,8},{1,5},{5,1},{9,13},{13,9},{2,6},{6,2},{1... | collective-permute-start | bytes 1474568 | tf_op jit(solution)/shard_map/ppermute | solution.py:129
  9.7 5.7 %collective-permute-start = (f32[16,512]{1,0:T(8,128)S(1)}, f32[16,512]{1,0:T(8,128)S(1)}, u32[]{:S(2)}, u32[]{:S(2)}) collective-permute-start(f32[16,512]{1,0:T(8,128)S(1)} %get-tuple-element.12), channel_id=1, source_target_pairs={{0,2},{1,3},{2,0},{3,1},{4,6},{5,7},{6,4},{7,5},{8,10},{9,11},{10,... | collective-permute-start | bytes 98312 | tf_op jit(solution)/shard_map/ppermute | solution.py:129
  13.6 7.5 %collective-permute-start.4 = (bf16[8,11264]{1,0:T(8,128)(2,1)S(1)}, bf16[8,11264]{1,0:T(8,128)(2,1)S(1)}, u32[]{:S(2)}, u32[]{:S(2)}) collective-permute-start(bf16[8,11264]{1,0:T(8,128)(2,1)S(1)} %pad_maximum_fusion), channel_id=1, source_target_pairs={{0,8},{4,12},{8,0},{12,4},{1,9},{5,13},{9,1},{13,5},{2,10},{6,14},... | collective-permute-start | bytes 540680 | tf_op jit(solution)/shard_map/ppermute | solution.py:129
  15.4 3.9 %collective-permute-start.2 = (f32[16,512]{1,0:T(8,128)S(1)}, f32[16,512]{1,0:T(8,128)S(1)}, u32[]{:S(2)}, u32[]{:S(2)}) collective-permute-start(f32[16,512]{1,0:T(8,128)S(1)} %add.41._.refs_0_), channel_id=1, source_target_pairs={{0,1},{1,0},{2,3},{3,2},{4,5},{5,4},{6,7},{7,6},{8,9},{9,8},{10,11... | collective-permute-start | bytes 98312 | tf_op jit(solution)/shard_map/ppermute | solution.py:129
  19.7 1.4 %collective-permute-start.3 = (f32[16,2048]{1,0:T(8,128)S(1)}, f32[16,2048]{1,0:T(8,128)S(1)}, u32[]{:S(2)}, u32[]{:S(2)}) collective-permute-start(f32[16,2048]{1,0:T(8,128)S(1)} %shard_map.97), channel_id=1, source_target_pairs={{0,4},{4,0},{8,12},{12,8},{1,5},{5,1},{9,13},{13,9},{2,6},{6,2},{1... | collective-permute-start | bytes 393224 | tf_op jit(solution)/shard_map/ppermute | solution.py:129
  21.2 4.1 %collective-permute-start.5 = (bf16[16,2048]{1,0:T(8,128)(2,1)S(1)}, bf16[16,2048]{1,0:T(8,128)(2,1)S(1)}, u32[]{:S(2)}, u32[]{:S(2)}) collective-permute-start(bf16[16,2048]{1,0:T(8,128)(2,1)S(1)} %add.42), channel_id=1, source_target_pairs={{0,12},{4,8},{8,4},{12,0},{1,13},{5,9},{9,5},{13,1},{2,14},{6,10},... | collective-permute-start | bytes 196616 | tf_op jit(solution)/shard_map/ppermute | solution.py:129
  22.7 1.5 %collective-permute-start.6 = (f32[8,7168]{1,0:T(8,128)S(1)}, f32[8,7168]{1,0:T(8,128)S(1)}, u32[]{:S(2)}, u32[]{:S(2)}) collective-permute-start(f32[8,7168]{1,0:T(8,128)S(1)} %slice_add_fusion), channel_id=1, source_target_pairs={{0,4},{4,0},{8,12},{12,8},{1,5},{5,1},{9,13},{13,9},{2,6},{6,2},{1... | collective-permute-start | bytes 688136 | tf_op jit(solution)/shard_map/ppermute | solution.py:129
